TPU v7x, 128 devices: a whole 4x4x4 slice. The times are simulated.
128 devices in a mesh: dp: 4 (over y), tok: 32 (over x, z, core).
Axes of the slice: x: 4, y: 4, z: 4, core: 2. Of those that a mesh axis runs over, the one named last changes fastest.
Arguments:
- q_tokens: bfloat16 [4, 16384, 1152], P('dp', 'tok'), may hold values from -8 to 8
- k_tokens: bfloat16 [4, 16384, 1152], P('dp', 'tok'), may hold values from -8 to 8
- v_tokens: bfloat16 [4, 16384, 1152], P('dp', 'tok'), may hold values from -6 to 6
- d_attended: bfloat16 [4, 16384, 1152], P('dp', 'tok'), may hold values from -6 to 6
- w_out: bfloat16 [1152, 1152], replicated, may hold values from -0.1875 to 0.1875
- lengths: int32 [4, 64], P('dp'), may hold values from 1 to 4, 128 in all within a row
Outputs:
- attended: bfloat16 [4, 16384, 1152], P('dp', 'tok')
- grad_q: bfloat16 [4, 16384, 1152], P('dp', 'tok')
- grad_k: bfloat16 [4, 16384, 1152], P('dp', 'tok')
- grad_v: bfloat16 [4, 16384, 1152], P('dp', 'tok')
- grad_wo: float32 [1152, 1152], P('tok')
All inputs are finite; a program needn't handle non-finite values.
Results may differ from a plain program's by a relative error of at most 0.025.
Values may be sent and summed in bfloat16 or wider, within the bound.
A program may use at most 256 MiB of HBM per device.

v0:
```python
import math

import jax
import jax.numpy as jnp
from jax import lax
from jax.sharding import PartitionSpec as P

HEADS = 16
HEAD_DIM = 72
BLOCK = 128
MOST = 4


masked_score = -1e30


def from_behind(value, axis, steps):
    count = lax.axis_size(axis)
    leading, last = (max(0, -steps), min(count, count - steps))
    return lax.ppermute(value, axis, [(source, source + steps) for source in range(leading, last)])


def block_facts(lengths, first_block, count, blk_dev):
    ends = jnp.cumsum(lengths)
    blocks = first_block + jnp.arange(count, dtype=jnp.int32)
    before = ends[None, :] <= blocks[:, None]
    image = jnp.sum(before.astype(jnp.int32), axis=1)
    start = jnp.sum(jnp.where(before, lengths[None, :], 0), axis=1)
    return (image, start, start // blk_dev)


def pad_tail(values):
    return jnp.pad(values, ((0, (MOST - 1) * BLOCK), (0, 0)))


def window_rows(values, win_idx):
    slots = win_idx.shape[0]
    blocks = pad_tail(values).reshape(-1, BLOCK, values.shape[1])
    picked = jnp.take(blocks, win_idx, axis=0)
    return picked.reshape(slots, MOST * BLOCK, HEADS, HEAD_DIM)


def slot_split(values):
    return values.reshape(values.shape[0] // BLOCK, BLOCK, HEADS, HEAD_DIM)


def all_scores(q_heads, k_win, same, scale):
    scores = (
        jnp.einsum("sqhd,skhd->shqk", q_heads, k_win, preferred_element_type=jnp.float32) * scale
    )
    return jnp.where(same[:, None, None, :], scores, masked_score)


def attention_forward(q_buf, k_buf, v_buf, win_idx, same):
    scale = HEAD_DIM ** (-0.5)
    total, width = q_buf.shape
    scores = all_scores(slot_split(q_buf), window_rows(k_buf, win_idx), same, scale)
    top = jnp.max(scores, axis=3, keepdims=True)
    lses = top + jnp.log(jnp.sum(jnp.exp(scores - top), axis=3, keepdims=True))
    probs_low = jnp.exp(scores - lses).astype(jnp.bfloat16)
    mixed = jnp.einsum(
        "shqk,skhd->sqhd",
        probs_low,
        window_rows(v_buf, win_idx),
        preferred_element_type=jnp.float32,
    )
    return (mixed.astype(jnp.bfloat16).reshape(total, width), lses)


def scatter_windows(parts, win_idx, total, width):
    slots = win_idx.shape[0]
    count = slots + MOST - 1
    picker = (win_idx[:, :, None] == jnp.arange(count, dtype=jnp.int32)[None, None, :]).astype(
        jnp.float32
    )
    parts = parts.reshape(slots, MOST, BLOCK * width)
    summed = jnp.einsum(
        "smb,smr->br",
        picker,
        parts,
        precision=lax.Precision.HIGHEST,
        preferred_element_type=jnp.float32,
    )
    return summed.reshape(count * BLOCK, width)[:total].astype(jnp.bfloat16)


def attention_backward(q_buf, k_buf, v_buf, mixed_buf, dm_buf, lses, win_idx, same):
    scale = HEAD_DIM ** (-0.5)
    total, width = q_buf.shape
    q_heads = slot_split(q_buf)
    dm_heads = slot_split(dm_buf)
    k_win = window_rows(k_buf, win_idx)
    v_win = window_rows(v_buf, win_idx)
    scores = all_scores(q_heads, k_win, same, scale)
    probs = jnp.exp(scores - lses)
    probs_low = probs.astype(jnp.bfloat16)
    d_probs = jnp.einsum("sqhd,skhd->shqk", dm_heads, v_win, preferred_element_type=jnp.float32)
    delta = jnp.einsum(
        "sqhd,sqhd->shq", dm_heads, slot_split(mixed_buf), preferred_element_type=jnp.float32
    )
    d_scores = (probs * (d_probs - delta[:, :, :, None])).astype(jnp.bfloat16)
    grad_q = (
        jnp.einsum("shqk,skhd->sqhd", d_scores, k_win, preferred_element_type=jnp.float32) * scale
    )
    dk_part = (
        jnp.einsum("shqk,sqhd->skhd", d_scores, q_heads, preferred_element_type=jnp.float32) * scale
    )
    dv_part = jnp.einsum("shqk,sqhd->skhd", probs_low, dm_heads, preferred_element_type=jnp.float32)
    grad_k = scatter_windows(dk_part, win_idx, total, width)
    grad_v = scatter_windows(dv_part, win_idx, total, width)
    return (grad_q.astype(jnp.bfloat16).reshape(total, width), grad_k, grad_v)


def reduce_weight(mixed_rows, dy_rows, norm):
    full = lax.dot_general(
        mixed_rows, dy_rows, (((0,), (0,)), ((), ())), preferred_element_type=jnp.float32
    )
    whole = lax.psum(full.astype(jnp.bfloat16), "dp")
    summed = lax.psum_scatter(whole, "tok", scatter_dimension=0, tiled=True).astype(jnp.float32)
    return summed * norm


def on_device(q_tokens, k_tokens, v_tokens, d_attended, w_out, lengths):
    rows = q_tokens.shape[1]
    blk_dev = rows // BLOCK
    tail = (MOST - 1) * BLOCK
    slots = blk_dev + MOST - 1
    norm = 1.0 / math.sqrt(lax.axis_size("dp") * lax.axis_size("tok") * rows)
    device = lax.axis_index("tok")
    first_block = device * blk_dev
    own_image, own_start, own_owner = block_facts(lengths[0], first_block, blk_dev, blk_dev)
    next_image, next_start, next_owner = block_facts(
        lengths[0], first_block + blk_dev, MOST - 1, blk_dev
    )
    slot_mine = jnp.concatenate([own_owner, next_owner]) == device
    slot_range = jnp.arange(slots, dtype=jnp.int32)
    slot_ids = jnp.where(slot_mine, jnp.concatenate([own_image, next_image]), -1 - slot_range)
    slot_start = jnp.where(
        slot_mine, jnp.concatenate([own_start, next_start]) - first_block, slot_range
    )
    win_idx = slot_start[:, None] + jnp.arange(MOST, dtype=jnp.int32)[None, :]
    pad_ids = jnp.concatenate([slot_ids, -1 - slots - jnp.arange(MOST - 1, dtype=jnp.int32)])
    key_ids = jnp.repeat(jnp.take(pad_ids, win_idx, axis=0), BLOCK, axis=1)
    same = slot_ids[:, None] == key_ids
    from_prev = jnp.repeat(own_owner != device, BLOCK)[:, None]
    q_own = q_tokens[0]
    k_own = k_tokens[0]
    v_own = v_tokens[0]
    dy_own = d_attended[0]
    transposed = (((1,), (1,)), ((), ()))

    def settle(local, returned):
        padded = jnp.pad(returned, ((0, local.shape[0] - returned.shape[0]), (0, 0)))
        return jnp.where(from_prev, padded, local)

    d_mixed = lax.dot_general(dy_own, w_out, transposed, preferred_element_type=jnp.float32).astype(
        jnp.bfloat16
    )
    incoming = from_behind((q_own[:tail], k_own[:tail], v_own[:tail], d_mixed[:tail]), "tok", -1)
    q_buf = jnp.concatenate([q_own, incoming[0]])
    k_buf = jnp.concatenate([k_own, incoming[1]])
    v_buf = jnp.concatenate([v_own, incoming[2]])
    dm_buf = jnp.concatenate([d_mixed, incoming[3]])
    mixed_buf, lses = attention_forward(q_buf, k_buf, v_buf, win_idx, same)
    gq_buf, gk_buf, gv_buf = attention_backward(
        q_buf, k_buf, v_buf, mixed_buf, dm_buf, lses, win_idx, same
    )
    returned = from_behind(
        (mixed_buf[rows:], gq_buf[rows:], gk_buf[rows:], gv_buf[rows:]), "tok", 1
    )
    mixed_home = settle(mixed_buf[:rows], returned[0])
    attended = jnp.dot(mixed_home, w_out, preferred_element_type=jnp.float32).astype(jnp.bfloat16)
    grad_rows = reduce_weight(mixed_home, dy_own, norm)
    grad_q = settle(gq_buf[:rows], returned[1])
    grad_k = settle(gk_buf[:rows], returned[2])
    grad_v = settle(gv_buf[:rows], returned[3])
    return (attended[None], grad_q[None], grad_k[None], grad_v[None], grad_rows)


def solution(mesh):
    in_specs = (
        P("dp", "tok", None),
        P("dp", "tok", None),
        P("dp", "tok", None),
        P("dp", "tok", None),
        P(),
        P("dp", None),
    )
    out_specs = (
        P("dp", "tok", None),
        P("dp", "tok", None),
        P("dp", "tok", None),
        P("dp", "tok", None),
        P("tok", None),
    )
    return jax.shard_map(
        on_device, mesh=mesh, in_specs=in_specs, out_specs=out_specs, check_vma=False
    )
```

profile of v0, /device:TPU:0, one launch (start us, length us, event | category | flops | bytes accessed | tf_op | source)
XLA Modules:
  0.0 682.0 jit_solution(2144073307391959002)
XLA Ops:
  41.1 5.1 reshape.267
  49.2 8.6 %reshape.313 = bf16[7,128,16,72]{3,2,1,0:T(8,128)(2,1)} reshape(bf16[896,1152]{1,0:T(8,128)(2,1)} %pad_maximum_fusion) | data formatting | bytes 4128768 | tf_op jit(solution)/shard_map/reshape | solution.py:44
  57.8 6.0 copy.71
  67.2 7.0 %gather_fusion.1 = bf16[28,128,1152]{2,1,0:T(8,128)(2,1)} fusion(bf16[10,128,1152]{2,1,0:T(8,128)(2,1)} %bitcast.110, s32[1024]{0:T(1024)S(1)} %pad_clamp_fusion.1), kind=kCustom, calls=%fused_computation.clone | custom fusion | bytes 16515184 | tf_op jit(solution)/shard_map/jit(_take)/gather | solution.py:39
  74.2 14.8 %copy.68 = bf16[7,4,128,1152]{2,1,3,0:T(4,128)(2,1)} copy(bf16[7,4,128,1152]{3,2,1,0:T(8,128)(2,1)} %bitcast.112) | data formatting | bytes 16515072 | tf_op jit(solution)/shard_map/jit(_take)/gather | solution.py:39
  89.0 4.4 bitcast_convert_fusion
  95.2 7.0 %gather_fusion.2 = bf16[28,128,1152]{2,1,0:T(8,128)(2,1)} fusion(bf16[10,128,1152]{2,1,0:T(8,128)(2,1)} %bitcast.109, s32[1024]{0:T(1024)S(1)} %pad_clamp_fusion.1), kind=kCustom, calls=%fused_computation.1.clone | custom fusion | bytes 16515184 | tf_op jit(solution)/shard_map/jit(_take)/gather | solution.py:39
  102.2 14.8 %copy.70 = bf16[7,4,128,1152]{2,1,3,0:T(4,128)(2,1)} copy(bf16[7,4,128,1152]{3,2,1,0:T(8,128)(2,1)} %bitcast.111) | data formatting | bytes 16515072 | tf_op jit(solution)/shard_map/jit(_take)/gather | solution.py:39
  117.0 16.8 %broadcast_select_fusion = (bf16[7,4,128,1152]{2,1,3,0:T(4,128)(2,1)}, bf16[7,4,128,1152]{2,1,3,0:T(4,128)(2,1)}) fusion(bf16[7,4,128,1152]{2,1,3,0:T(4,128)(2,1)} %copy.70, pred[7,4]{1,0:T(8,128)(4,1)S(1)} %copy-done.14, bf16[7,4,128,1152]{2,1,3,0:T(4,128)(2,1)} %copy.68), kind=kLoop, calls=%fused_computation.16 | loop fusion | flops 8257536 | bytes 33030172 | tf_op jit(solution)/shard_map/jit(_take)/select_n | solution.py:39
  133.9 14.2 %reshape.266 = bf16[7,512,16,72]{1,3,2,0:T(8,128)(2,1)} reshape(bf16[7,4,128,1152]{2,1,3,0:T(4,128)(2,1)} %get-tuple-element.29) | data formatting | bytes 16515072 | tf_op jit(solution)/shard_map/reshape | solution.py:40
  148.1 14.3 %reshape.262 = bf16[7,512,16,72]{1,3,2,0:T(8,128)(2,1)} reshape(bf16[7,4,128,1152]{2,1,3,0:T(4,128)(2,1)} %get-tuple-element.30) | data formatting | bytes 16515072 | tf_op jit(solution)/shard_map/reshape | solution.py:40
  162.4 15.5 %fusion.4 = (f32[7,16,128]{2,1,0:T(8,128)S(1)}, f32[7,16,128,512]{3,2,1,0:T(8,128)}) fusion(pred[7,512]{1,0:T(8,128)(4,1)S(1)} %bitcast_compare_fusion, bf16[7,128,16,72]{1,3,2,0:T(8,128)(2,1)} %copy.71, bf16[7,512,16,72]{1,3,2,0:T(8,128)(2,1)} %reshape.266), kind=kOutput, calls=%fused_computation.12 | convolution fusion | flops 1078970368 | bytes 39742976 | tf_op jit(solution)/shard_map/sqhd,skhd->shqk/dot_general | solution.py:49
  177.9 13.4 %exponential_reduce_fusion = f32[7,16,128]{2,1,0:T(8,128)S(1)} fusion(f32[7,16,128,512]{3,2,1,0:T(8,128)} %get-tuple-element.38, f32[7,16,128]{2,1,0:T(8,128)S(1)} %get-tuple-element.37, pred[7,512]{1,0:T(8,128)(4,1)S(1)} %bitcast_compare_fusion), kind=kLoop, calls=%fused_computation.9 | loop fusion | flops 29345792 | bytes 29478400 | tf_op jit(solution)/shard_map/reduce_sum | solution.py:59
  191.4 17.0 %multiply_reduce_fusion = (f32[7,16,128]{2,1,0:T(8,128)}, bf16[7,16,72,128]{3,2,1,0:T(8,128)(2,1)S(1)}) fusion(f32[7,16,128,72]{2,0,3,1:T(8,128)} %bitcast_convert_fusion, bf16[7,512,16,72]{1,3,2,0:T(8,128)(2,1)} %reshape.262, f32[7,16,128,512]{3,2,1,0:T(8,128)} %get-tuple-element.38, f32[7,16,128]{2,1,0:T(8,128)S(1)} %log_add_fusion, ...), kind=kOutput, calls=%fused_computation.25 | convolution fusion | flops 1090439168 | bytes 43929088 | tf_op jit(solution)/shard_map/shqk,skhd->sqhd/dot_general | solution.py:61
  209.5 17.4 %convolution_bitcast_fusion.2 = f32[7,512,16,72]{1,3,2,0:T(8,128)} fusion(bf16[7,128,16,72]{1,0,3,2:T(8,128)(2,1)} %reshape.267, f32[7,16,128,512]{3,2,1,0:T(8,128)} %get-tuple-element.38, f32[7,16,128]{2,1,0:T(8,128)} %copy-done.9, pred[7,512]{1,0:T(8,128)(4,1)S(1)} %bitcast_compare_fusion), kind=kOutput, calls=%fused_computation.18 | convolution fusion | flops 1086324736 | bytes 48000512 | tf_op jit(solution)/shard_map/shqk,sqhd->skhd/dot_general | solution.py:108
  226.9 21.0 %multiply_convert_fusion = bf16[7,16,128,512]{3,2,1,0:T(8,128)(2,1)} fusion(f32[7,16,128,512]{3,2,1,0:T(8,128)} %get-tuple-element.38, f32[7,16,128]{2,1,0:T(8,128)} %get-tuple-element.39, f32[7,16,128]{2,1,0:T(8,128)} %copy-done.9, pred[7,512]{1,0:T(8,128)(4,1)S(1)} %bitcast_compare_fusion, bf16[7,512,16,72]{1,3,2,0:T(8,128)(2,1)} %reshape.262, ...), kind=kOutput, calls=%fused_computation.7 | convolution fusion | flops 1101004800 | bytes 54480384 | tf_op jit(solution)/shard_map/sqhd,skhd->shqk/dot_general | solution.py:97
  247.9 10.7 %fusion.14 = bf16[7,128,16,72]{1,3,2,0:T(8,128)(2,1)S(1)} fusion(bf16[7,512,16,72]{1,3,2,0:T(8,128)(2,1)} %reshape.266, bf16[7,16,128,512]{3,2,1,0:T(8,128)(2,1)} %multiply_convert_fusion), kind=kOutput, calls=%fused_computation.33 | convolution fusion | flops 1059028992 | bytes 25001984 | tf_op jit(solution)/shard_map/shqk,skhd->sqhd/dot_general | solution.py:103
  258.6 14.2 %multiply_bitcast_fusion = f32[7,512,16,72]{1,3,2,0:T(8,128)} fusion(bf16[7,128,16,72]{1,3,2,0:T(8,128)(2,1)S(1)} %copy-done.1, bf16[7,16,128,512]{3,2,1,0:T(8,128)(2,1)} %multiply_convert_fusion), kind=kOutput, calls=%fused_computation.15 | convolution fusion | flops 1061093376 | bytes 33259520 | tf_op jit(solution)/shard_map/shqk,sqhd->skhd/dot_general | solution.py:106
  276.5 21.9 %collective-permute-start.3 = (bf16[384,1152]{0,1:T(8,128)(2,1)}, bf16[384,1152]{0,1:T(8,128)(2,1)}, u32[]{:S(2)}, u32[]{:S(2)}) collective-permute-start(bf16[384,1152]{0,1:T(8,128)(2,1)} %bitcast.108), channel_id=1, source_target_pairs={{0,1},{1,2},{2,3},{3,4},{4,5},{5,6},{6,7},{7,8},{8,9},{9,10},{10,1... | collective-permute-start | bytes 2654216 | tf_op jit(solution)/shard_map/ppermute | solution.py:20
  302.6 27.5 %copy.80 = f32[7,512,16,72]{3,2,1,0:T(8,128)} copy(f32[7,512,16,72]{1,3,2,0:T(8,128)} %multiply_bitcast_fusion) | data formatting | bytes 33030144 | tf_op jit(solution)/shard_map/mul | solution.py:106
  330.1 28.4 %reshape.268 = f32[7,4,147456]{2,1,0:T(4,128)} reshape(f32[7,512,16,72]{3,2,1,0:T(8,128)} %copy.80) | data formatting | bytes 33030144 | tf_op jit(solution)/shard_map/reshape | solution.py:76
  358.4 27.6 %fusion.1 = bf16[10,147456]{1,0:T(8,128)(2,1)S(1)} fusion(f32[7,4,147456]{2,1,0:T(4,128)} %reshape.268, s32[7,4]{0,1:T(4,128)S(1)} %copy-done.10), kind=kOutput, calls=%fused_computation.5 | convolution fusion | flops 496927008 | bytes 19464304 | tf_op jit(solution)/shard_map/smb,smr->br/dot_general | solution.py:77
  397.1 27.6 %copy.85 = f32[7,512,16,72]{3,2,1,0:T(8,128)} copy(f32[7,512,16,72]{1,3,2,0:T(8,128)} %convolution_bitcast_fusion.2) | data formatting | bytes 33030144 | tf_op jit(solution)/shard_map/shqk,sqhd->skhd/transpose | solution.py:108
  424.6 28.3 %reshape.269 = f32[7,4,147456]{2,1,0:T(4,128)} reshape(f32[7,512,16,72]{3,2,1,0:T(8,128)} %copy.85) | data formatting | bytes 33030144 | tf_op jit(solution)/shard_map/reshape | solution.py:76
  453.0 27.6 %fusion.2 = bf16[10,147456]{1,0:T(8,128)(2,1)S(1)} fusion(f32[7,4,147456]{2,1,0:T(4,128)} %reshape.269, s32[7,4]{0,1:T(4,128)S(1)} %copy-done.10), kind=kOutput, calls=%fused_computation.6 | convolution fusion | flops 496927008 | bytes 19464304 | tf_op jit(solution)/shard_map/smb,smr->br/dot_general | solution.py:77
  490.5 5.2 convolution_convert_fusion
  495.6 77.9 %fusion = bf16[48,1152]{1,0:T(8,128)(2,1)S(1)} fusion(bf16[1152,1152]{1,0:T(8,128)(2,1)} %convolution_convert_fusion), kind=kCustom, calls=%all-reduce-scatter | all-reduce-scatter fusion | flops 1769473 | bytes 2765312
  603.9 6.5 collective-permute-start.9
  614.0 4.9 select_bitcast_fusion
  618.9 13.3 %concatenate.47 = bf16[420,1152]{1,0:T(8,128)(2,1)} concatenate(bf16[36,1152]{1,0:T(8,128)(2,1)} %collective-permute-done.15, bf16[48,1152]{1,0:T(8,128)(2,1)S(1)} %collective-permute-done.14, bf16[48,1152]{1,0:T(8,128)(2,1)S(1)} %collective-permute-done.13, bf16[48,1152]{1,0:T(8,128)(2,1)S(1)} %collective-permute-done.12, bf16[48,1152]{1,0:T(8,128)(2,1)S(1)} %collective-permute-done.11, ...), dimensions={0} | concatenate | bytes 1935360
  633.8 4.4 fusion.13
  645.4 27.8 %all-reduce.10.cloned.1.call-done = bf16[36,1152]{1,0:T(8,128)(2,1)} async-done(((bf16[36,1152]{1,0:T(8,128)(2,1)}), bf16[36,1152]{1,0:T(8,128)(2,1)}) %all-reduce.10.cloned.1.call-update) | async-done | bytes 82960 | tf_op jit(solution)/shard_map/psum | solution.py:118
  (134 shorter events, 115.3 us)
Async XLA Ops:
  7.2 9.5 %copy-start = (bf16[1152,1152]{1,0:T(8,128)(2,1)S(1)}, bf16[1152,1152]{1,0:T(8,128)(2,1)}, u32[]{:S(2)}) copy-start(bf16[1152,1152]{1,0:T(8,128)(2,1)} %param.12) | copy-start | bytes 7962628
  7.2 666.0 %all-reduce.10.cloned.1.call-start = ((), (), s32[]{:S(2)}) async-start(), calls=%async_computation | async-start | bytes 184320 | tf_op jit(solution)/shard_map/psum | solution.py:118
  7.2 7.1 %copy-start.7 = (bf16[1,512,1152]{2,1,0:T(8,128)(2,1)S(1)}, bf16[1,512,1152]{2,1,0:T(8,128)(2,1)}, u32[]{:S(2)}) copy-start(bf16[1,512,1152]{2,1,0:T(8,128)(2,1)} %param.8) | copy-start | bytes 3538948
  7.2 9.5 %copy-start.17 = (bf16[1,512,1152]{2,1,0:T(8,128)(2,1)S(1)}, bf16[1,512,1152]{2,1,0:T(8,128)(2,1)}, u32[]{:S(2)}) copy-start(bf16[1,512,1152]{2,1,0:T(8,128)(2,1)} %param.11) | copy-start | bytes 3538948
  9.6 54.3 %collective-permute-start = (bf16[384,1152]{1,0:T(8,128)(2,1)}, bf16[384,1152]{1,0:T(8,128)(2,1)}, u32[]{:S(2)}, u32[]{:S(2)}) collective-permute-start(bf16[384,1152]{1,0:T(8,128)(2,1)} %slice_bitcast_fusion.2), channel_id=1, source_target_pairs={{1,0},{2,1},{3,2},{4,3},{5,4},{6,5},{7,6},{8,7},{9,8},{10,9},{11,1... | collective-permute-start | bytes 2654216 | tf_op jit(solution)/shard_map/ppermute | solution.py:20
  13.0 80.4 %collective-permute-start.2 = (bf16[384,1152]{1,0:T(8,128)(2,1)}, bf16[384,1152]{1,0:T(8,128)(2,1)S(1)}, u32[]{:S(2)}, u32[]{:S(2)}) collective-permute-start(bf16[384,1152]{1,0:T(8,128)(2,1)} %slice_bitcast_fusion), channel_id=1, source_target_pairs={{1,0},{2,1},{3,2},{4,3},{5,4},{6,5},{7,6},{8,7},{9,8},{10,9},{11,1... | collective-permute-start | bytes 2654216 | tf_op jit(solution)/shard_map/ppermute | solution.py:20
  15.3 7.2 %copy-start.11 = (s32[1,64]{1,0:T(1,128)S(1)}, s32[1,64]{1,0:T(1,128)}, u32[]{:S(2)}) copy-start(s32[1,64]{1,0:T(1,128)} %param.13) | copy-start | bytes 772
  15.3 30.9 %collective-permute-start.1 = (bf16[384,1152]{1,0:T(8,128)(2,1)}, bf16[384,1152]{1,0:T(8,128)(2,1)}, u32[]{:S(2)}, u32[]{:S(2)}) collective-permute-start(bf16[384,1152]{1,0:T(8,128)(2,1)} %slice_bitcast_fusion.1), channel_id=1, source_target_pairs={{1,0},{2,1},{3,2},{4,3},{5,4},{6,5},{7,6},{8,7},{9,8},{10,9},{11,1... | collective-permute-start | bytes 2654216 | tf_op jit(solution)/shard_map/ppermute | solution.py:20
  20.6 13.4 %collective-permute-start.4 = (bf16[384,1152]{1,0:T(8,128)(2,1)}, bf16[384,1152]{1,0:T(8,128)(2,1)}, u32[]{:S(2)}, u32[]{:S(2)}) collective-permute-start(bf16[384,1152]{1,0:T(8,128)(2,1)} %slice.110), channel_id=1, source_target_pairs={{1,0},{2,1},{3,2},{4,3},{5,4},{6,5},{7,6},{8,7},{9,8},{10,9},{11,1... | collective-permute-start | bytes 2654216 | tf_op jit(solution)/shard_map/ppermute | solution.py:20
  89.0 4.4 copy-start.6
  102.2 14.8 %copy-start.14 = (pred[7,4]{1,0:T(8,128)(4,1)S(1)}, pred[7,4]{1,0:T(8,128)(4,1)}, u32[]{:S(2)}) copy-start(pred[7,4]{1,0:T(8,128)(4,1)} %compare_and_fusion) | copy-start | bytes 88
  191.4 17.0 %copy-start.9 = (f32[7,16,128]{2,1,0:T(8,128)}, f32[7,16,128]{2,1,0:T(8,128)S(1)}, u32[]{:S(2)}) copy-start(f32[7,16,128]{2,1,0:T(8,128)S(1)} %log_add_fusion) | copy-start | bytes 172036
  247.9 10.7 %copy-start.1 = (bf16[7,128,16,72]{1,3,2,0:T(8,128)(2,1)S(1)}, bf16[7,128,16,72]{1,3,2,0:T(8,128)(2,1)}, u32[]{:S(2)}) copy-start(bf16[7,128,16,72]{1,3,2,0:T(8,128)(2,1)} %copy.71) | copy-start | bytes 6193156
  258.6 39.8 %copy-start.4 = (bf16[7,128,16,72]{1,3,2,0:T(8,128)(2,1)}, bf16[7,128,16,72]{1,3,2,0:T(8,128)(2,1)S(1)}, u32[]{:S(2)}) copy-start(bf16[7,128,16,72]{1,3,2,0:T(8,128)(2,1)S(1)} %fusion.14) | copy-start | bytes 6193156
  258.6 14.2 %copy-start.5 = (bf16[4,128,16,72]{1,3,2,0:T(8,128)(2,1)S(1)}, bf16[4,128,16,72]{1,3,2,0:T(8,128)(2,1)}, u32[]{:S(2)}) copy-start(bf16[4,128,16,72]{1,3,2,0:T(8,128)(2,1)} %slice.109) | copy-start | bytes 3538948
  276.5 213.9 %collective-permute-start.3 = (bf16[384,1152]{0,1:T(8,128)(2,1)}, bf16[384,1152]{0,1:T(8,128)(2,1)}, u32[]{:S(2)}, u32[]{:S(2)}) collective-permute-start(bf16[384,1152]{0,1:T(8,128)(2,1)} %bitcast.108), channel_id=1, source_target_pairs={{0,1},{1,2},{2,3},{3,4},{4,5},{5,6},{6,7},{7,8},{8,9},{9,10},{10,1... | collective-permute-start | bytes 2654216 | tf_op jit(solution)/shard_map/ppermute | solution.py:20
  300.3 275.8 %collective-permute-start.5 = (bf16[384,1152]{0,1:T(8,128)(2,1)}, bf16[384,1152]{0,1:T(8,128)(2,1)}, u32[]{:S(2)}, u32[]{:S(2)}) collective-permute-start(bf16[384,1152]{0,1:T(8,128)(2,1)} %bitcast.107), channel_id=1, source_target_pairs={{0,1},{1,2},{2,3},{3,4},{4,5},{5,6},{6,7},{7,8},{8,9},{9,10},{10,1... | collective-permute-start | bytes 2654216 | tf_op jit(solution)/shard_map/ppermute | solution.py:20
  330.1 28.4 %copy-start.10 = (s32[7,4]{0,1:T(4,128)S(1)}, s32[7,4]{0,1:T(4,128)}, u32[]{:S(2)}) copy-start(s32[7,4]{0,1:T(4,128)} %copy.78) | copy-start | bytes 340
  393.4 204.1 %collective-permute-start.6 = (bf16[384,1152]{0,1:T(8,128)(2,1)}, bf16[384,1152]{0,1:T(8,128)(2,1)}, u32[]{:S(2)}, u32[]{:S(2)}) collective-permute-start(bf16[384,1152]{0,1:T(8,128)(2,1)} %copy.82), channel_id=1, source_target_pairs={{0,1},{1,2},{2,3},{3,4},{4,5},{5,6},{6,7},{7,8},{8,9},{9,10},{10,1... | collective-permute-start | bytes 2654216 | tf_op jit(solution)/shard_map/ppermute | solution.py:20
  480.6 2.1 copy-start.3
  482.7 7.7 %copy-start.15 = (pred[512]{0:T(512)(128)(4,1)S(1)}, pred[512]{0:T(512)(128)(4,1)}, u32[]{:S(2)}) copy-start(pred[512]{0:T(512)(128)(4,1)} %broadcast_bitcast_fusion.1) | copy-start | bytes 1540
  488.0 110.8 %collective-permute-start.7 = (bf16[384,1152]{0,1:T(8,128)(2,1)}, bf16[384,1152]{0,1:T(8,128)(2,1)}, u32[]{:S(2)}, u32[]{:S(2)}) collective-permute-start(bf16[384,1152]{0,1:T(8,128)(2,1)} %copy.87), channel_id=1, source_target_pairs={{0,1},{1,2},{2,3},{3,4},{4,5},{5,6},{6,7},{7,8},{8,9},{9,10},{10,1... | collective-permute-start | bytes 2654216 | tf_op jit(solution)/shard_map/ppermute | solution.py:20
  490.4 87.6 %copy-start.16 = (u32[128]{0:T(128)S(1)}, u32[128]{0:T(128)}, u32[]{:S(2)}) copy-start(u32[128]{0:T(128)} %constant.97) | copy-start | bytes 1540
  573.5 30.4 %collective-permute-start.14 = (bf16[48,1152]{1,0:T(8,128)(2,1)S(1)}, bf16[48,1152]{1,0:T(8,128)(2,1)S(1)}, u32[]{:S(2)}, u32[]{:S(2)}) collective-permute-start(bf16[48,1152]{1,0:T(8,128)(2,1)S(1)} %fusion), channel_id=1, source_target_pairs={{0,7},{1,8},{2,9},{3,10},{4,11},{5,12},{6,13},{7,14},{8,15},{9,16}... | collective-permute-start | bytes 331784
  574.8 35.6 %collective-permute-start.13 = (bf16[48,1152]{1,0:T(8,128)(2,1)S(1)}, bf16[48,1152]{1,0:T(8,128)(2,1)S(1)}, u32[]{:S(2)}, u32[]{:S(2)}) collective-permute-start(bf16[48,1152]{1,0:T(8,128)(2,1)S(1)} %fusion), channel_id=1, source_target_pairs={{0,6},{1,7},{2,8},{3,9},{4,10},{5,11},{6,12},{7,13},{8,14},{9,15},... | collective-permute-start | bytes 331784
  576.1 26.4 %collective-permute-start.15 = (bf16[36,1152]{1,0:T(8,128)(2,1)S(1)}, bf16[36,1152]{1,0:T(8,128)(2,1)}, u32[]{:S(2)}, u32[]{:S(2)}) collective-permute-start(bf16[36,1152]{1,0:T(8,128)(2,1)S(1)} %slice.117), channel_id=1, source_target_pairs={{0,8},{1,9},{2,10},{3,11},{4,12},{5,13},{6,14},{7,15},{8,16},{9,17... | collective-permute-start | bytes 248840
  579.3 5.3 slice-start
  597.5 21.4 %collective-permute-start.12 = (bf16[48,1152]{1,0:T(8,128)(2,1)S(1)}, bf16[48,1152]{1,0:T(8,128)(2,1)S(1)}, u32[]{:S(2)}, u32[]{:S(2)}) collective-permute-start(bf16[48,1152]{1,0:T(8,128)(2,1)S(1)} %fusion), channel_id=1, source_target_pairs={{0,5},{1,6},{2,7},{3,8},{4,9},{5,10},{6,11},{7,12},{8,13},{9,14},{... | collective-permute-start | bytes 331784
  598.8 20.1 %collective-permute-start.11 = (bf16[48,1152]{1,0:T(8,128)(2,1)S(1)}, bf16[48,1152]{1,0:T(8,128)(2,1)S(1)}, u32[]{:S(2)}, u32[]{:S(2)}) collective-permute-start(bf16[48,1152]{1,0:T(8,128)(2,1)S(1)} %fusion), channel_id=1, source_target_pairs={{0,4},{1,5},{2,6},{3,7},{4,8},{5,9},{6,10},{7,11},{8,12},{9,13},{1... | collective-permute-start | bytes 331784
  602.6 16.3 %collective-permute-start.10 = (bf16[48,1152]{1,0:T(8,128)(2,1)S(1)}, bf16[48,1152]{1,0:T(8,128)(2,1)S(1)}, u32[]{:S(2)}, u32[]{:S(2)}) collective-permute-start(bf16[48,1152]{1,0:T(8,128)(2,1)S(1)} %fusion), channel_id=1, source_target_pairs={{0,3},{1,4},{2,5},{3,6},{4,7},{5,8},{6,9},{7,10},{8,11},{9,12},{10... | collective-permute-start | bytes 331784
  603.9 15.0 %collective-permute-start.9 = (bf16[48,1152]{1,0:T(8,128)(2,1)S(1)}, bf16[48,1152]{1,0:T(8,128)(2,1)S(1)}, u32[]{:S(2)}, u32[]{:S(2)}) collective-permute-start(bf16[48,1152]{1,0:T(8,128)(2,1)S(1)} %fusion), channel_id=1, source_target_pairs={{0,2},{1,3},{2,4},{3,5},{4,6},{5,7},{6,8},{7,9},{8,10},{9,11},{10,... | collective-permute-start | bytes 331784
  610.4 8.5 %collective-permute-start.8 = (bf16[48,1152]{1,0:T(8,128)(2,1)S(1)}, bf16[48,1152]{1,0:T(8,128)(2,1)S(1)}, u32[]{:S(2)}, u32[]{:S(2)}) collective-permute-start(bf16[48,1152]{1,0:T(8,128)(2,1)S(1)} %fusion), channel_id=1, source_target_pairs={{0,1},{1,2},{2,3},{3,4},{4,5},{5,6},{6,7},{7,8},{8,9},{9,10},{10,1... | collective-permute-start | bytes 331784
  (4 other events, 4.3 us)
Sparse Core Ops, SparseCore 0:
  634.0 39.1 all-reduce.9
where the time goes:
time: 695 us; the launch traced here: 682 us
  local copies, waits for them, and re-layouts  282 us (41%)
  matrix products  162 us (23%)
  blocking collectives  77.9 us (11%)
  other arithmetic  59.7 us (9%)
  starting transfers between devices  56.4 us (8%)
  waiting for transfers between devices  27.9 us (4%)
  between operations  15.6 us (2%)
    unnamed x1, blocking collectives  77.9 us
    reshape x2, local copies, waits for them, and re-layouts, scatter_windows(): parts = parts.reshape(slots, MOST, BLOCK * width)  56.7 us
    dot_general x2, matrix products, scatter_windows(): jnp.einsum('smb,smr->br', picker, parts, precision=lax.Precision.HIGHEST,...  55.3 us
    gather x4, local copies, waits for them, and re-layouts, window_rows(): picked = jnp.take(blocks, win_idx, axis=0)  43.7 us
    ppermute x8, starting transfers between devices, from_behind(): lax.ppermute(value, axis, [(source, source + steps) for source in range(l...  35.5 us
    unnamed x46, local copies, waits for them, and re-layouts  31.2 us
    reshape x2, local copies, waits for them, and re-layouts, window_rows(): return picked.reshape(slots, MOST * BLOCK, HEADS, HEAD_DIM)  28.5 us
    psum x1, waiting for transfers between devices, reduce_weight(): whole = lax.psum(full.astype(jnp.bfloat16), 'dp')  27.8 us
  transfers between devices with their start and end apart: 17, of which 1 were waited for; matrix products, arithmetic and copies ran while one was open for 55% of the time, Pallas kernels for 0%

commit v1 on v0

v1 whole, which is shorter than its diff:
```python
import functools
import math

import jax
import jax.numpy as jnp
from jax import lax
from jax.experimental import pallas as pl
from jax.experimental.pallas import tpu as pltpu
from jax.sharding import PartitionSpec as P

HEADS = 16
HEAD_DIM = 72
BLOCK = 128
D = 1152
OWN = 4
SLOTS = 8
WINDOW = 256
SCALE = HEAD_DIM ** (-0.5)
EXP2_SCALE = SCALE * math.log2(math.e)
MESH = pl.DeviceIdType.MESH
NN = (((1,), (0,)), ((), ()))
NT = (((1,), (1,)), ((), ()))
TN = (((0,), (0,)), ((), ()))


def dot(a, b, dims):
    return lax.dot_general(a, b, dims, preferred_element_type=jnp.float32)


def boundary(lengths_ref, edge):
    def step(i, carry):
        start, before, after = carry
        end = start + lengths_ref[0, i]
        hit = jnp.logical_and(start < edge, end > edge)
        return (end, jnp.where(hit, edge - start, before), jnp.where(hit, end - edge, after))

    zero = jnp.int32(0)
    _, before, after = lax.fori_loop(0, lengths_ref.shape[1], step, (zero, zero, zero))
    return before, after


def greet(left, right):
    barrier = pltpu.get_barrier_semaphore()
    for other in (left, right):
        pl.semaphore_signal(barrier, inc=1, device_id={"tok": other}, device_id_type=MESH)
    pl.semaphore_wait(barrier, 2)


def ring_neighbours(count):
    me = lax.axis_index("tok")
    return lax.rem(me + count - 1, count), lax.rem(me + 1, count)


def exchange_kernel(
    count, lengths_ref, q_ref, k_ref, v_ref, dy_ref, w_ref, halo_ref, dm_ref, pack, send_sem, recv_sem
):
    left, right = ring_neighbours(count)
    first = lax.axis_index("tok") * OWN
    greet(left, right)
    copies = []

    def send(side, slot, source):
        copy = pltpu.make_async_remote_copy(
            src_ref=source,
            dst_ref=halo_ref.at[1 - side, slot],
            send_sem=send_sem.at[side, slot],
            recv_sem=recv_sem.at[1 - side, slot],
            device_id={"tok": right if side else left},
            device_id_type=MESH,
        )
        copy.start()
        copies.append(copy)

    near = [slice(0, BLOCK), slice(3 * BLOCK, 4 * BLOCK)]
    far = [slice(BLOCK, 2 * BLOCK), slice(2 * BLOCK, 3 * BLOCK)]
    for side in range(2):
        send(side, 0, k_ref.at[near[side]])
        send(side, 1, v_ref.at[near[side]])
    for side in range(2):
        before, after = boundary(lengths_ref, first + side * OWN)
        shared = jnp.logical_and(before == 2, after == 2)
        pack[side, 0] = jnp.where(shared, k_ref[far[side]], q_ref[near[side]])
        pack[side, 1] = jnp.where(shared, v_ref[far[side]], dy_ref[near[side]])
        send(side, 2, pack.at[side, 0])
        send(side, 3, pack.at[side, 1])
    for part in range(OWN):
        rows = slice(part * BLOCK, (part + 1) * BLOCK)
        dm_ref[rows] = dot(dy_ref[rows], w_ref[...], NT).astype(jnp.bfloat16)
    for copy in copies:
        copy.wait()


def attend(q_buf, k_buf, v_buf, dm_buf, mixed, gq, gk, gv, q_at, q_blocks, k_at, k_blocks):
    q_rows = pl.ds(pl.multiple_of(q_at * BLOCK, BLOCK), q_blocks * BLOCK)
    k_rows = pl.ds(pl.multiple_of(k_at * BLOCK, BLOCK), k_blocks * BLOCK)
    lane = lax.broadcasted_iota(jnp.int32, (1, WINDOW), 1)

    def head(h):
        at = h * HEAD_DIM
        base = jnp.minimum(at // 128, (D - WINDOW) // 128) * 128
        offset = at - base
        window = pl.ds(pl.multiple_of(base, 128), WINDOW)
        inside = jnp.logical_and(lane >= offset, lane < offset + HEAD_DIM)
        keep = jnp.where(inside, 1.0, 0.0).astype(jnp.bfloat16)
        q = q_buf[q_rows, window]
        k = k_buf[k_rows, window]
        v = v_buf[k_rows, window]
        dm = dm_buf[q_rows, window]
        scores = dot(k * keep, q, NT)
        d_probs = dot(v * keep, dm, NT)
        top = jnp.max(scores, axis=0, keepdims=True)
        weights = jnp.exp2((scores - top) * EXP2_SCALE)
        probs = weights * (1.0 / jnp.sum(weights, axis=0, keepdims=True))
        probs_low = probs.astype(jnp.bfloat16)
        product = probs * d_probs
        delta = jnp.sum(product, axis=0, keepdims=True)
        d_scores = (product - probs * delta).astype(jnp.bfloat16)

        def put(ref, rows, new):
            old = ref[rows, window]
            ref[rows, window] = jnp.where(lane < offset, old, new.astype(jnp.bfloat16))

        put(mixed, q_rows, dot(probs_low, v, TN))
        put(gv, k_rows, dot(probs_low, dm, NN))
        put(gq, q_rows, dot(d_scores, k, TN) * SCALE)
        put(gk, k_rows, dot(d_scores, q, NN) * SCALE)

    def two(i, carry):
        head(2 * i)
        head(2 * i + 1)
        return carry

    lax.fori_loop(0, HEADS // 2, two, 0)


def attention_kernel(
    lengths_ref, q_ref, k_ref, v_ref, dy_ref, dm_ref, halo_ref, w_ref,
    att_out, gq_out, gk_out, gv_out, ret_out, gw_out, flags_out,
    q_buf, k_buf, v_buf, dy_buf, dm_buf, w_buf, mixed, gq, gk, gv, att, gw_buf, work, sem,
):
    first = lax.axis_index("tok") * OWN
    last = first + OWN
    own = pl.ds(2 * BLOCK, OWN * BLOCK)

    def block(i):
        return pl.ds(i * BLOCK, BLOCK)

    loads = [
        (q_ref, q_buf.at[own]), (k_ref, k_buf.at[own]), (v_ref, v_buf.at[own]),
        (dm_ref, dm_buf.at[own]), (dy_ref, dy_buf.at[own]), (w_ref, w_buf),
    ]
    for side, (near, far) in enumerate(((1, 0), (6, 7))):
        loads += [
            (halo_ref.at[side, 0], k_buf.at[block(near)]),
            (halo_ref.at[side, 1], v_buf.at[block(near)]),
            (halo_ref.at[side, 2], q_buf.at[block(near)]),
            (halo_ref.at[side, 2], k_buf.at[block(far)]),
            (halo_ref.at[side, 3], dy_buf.at[block(near)]),
            (halo_ref.at[side, 3], v_buf.at[block(far)]),
        ]
    copies = [pltpu.make_async_copy(a, b, sem.at[i]) for i, (a, b) in enumerate(loads)]
    for copy in copies:
        copy.start()

    l_before, l_after = boundary(lengths_ref, first)
    r_before, r_after = boundary(lengths_ref, last)
    l_shared = jnp.logical_and(l_before == 2, l_after == 2)
    r_shared = jnp.logical_and(r_before == 2, r_after == 2)
    l_away = l_after == 1
    l_here = jnp.logical_and(l_before == 1, l_after > 1)
    r_here = r_after == 1
    r_away = jnp.logical_and(r_before == 1, r_after > 1)
    for i, flag in enumerate((l_away, l_shared, r_away, r_shared)):
        flags_out[i] = flag.astype(jnp.int32)

    def collect(i, carry):
        start, number = carry
        end = start + lengths_ref[0, i]
        on_left = jnp.logical_and(start < first, end > first)
        on_right = jnp.logical_and(start < last, end > last)
        within = jnp.logical_and(start >= first, end <= last)
        mine = jnp.logical_or(
            within,
            jnp.logical_or(
                jnp.logical_and(on_left, jnp.logical_not(l_away)),
                jnp.logical_and(on_right, jnp.logical_not(r_away)),
            ),
        )
        shared = jnp.logical_or(
            jnp.logical_and(on_left, l_shared), jnp.logical_and(on_right, r_shared)
        )

        @pl.when(mine)
        def _():
            work[number, 0] = jnp.where(shared, 5, end - start)
            work[number, 1] = start - first + 2

        return end, number + mine.astype(jnp.int32)

    _, number = lax.fori_loop(
        0, lengths_ref.shape[1], collect, (jnp.int32(0), jnp.int32(0))
    )
    for copy in copies:
        copy.wait()

    for here, slot in ((l_here, 1), (r_here, 6)):
        @pl.when(here)
        def _():
            dm_buf[block(slot)] = dot(dy_buf[block(slot)], w_buf[...], NT).astype(jnp.bfloat16)

    bufs = (q_buf, k_buf, v_buf, dm_buf, mixed, gq, gk, gv)

    def image(i, carry):
        kind, at = work[i, 0], work[i, 1]
        for blocks in range(1, OWN + 1):
            @pl.when(kind == blocks)
            def _():
                attend(*bufs, at, blocks, at, blocks)

        @pl.when(kind == 5)
        def _():
            attend(*bufs, jnp.where(at == 0, 2, 4), 2, at, 4)

        return carry

    lax.fori_loop(0, number, image, 0)

    idle = (
        (jnp.logical_not(l_here), 1), (l_away, 2), (r_away, 5), (jnp.logical_not(r_here), 6)
    )
    for flag, slot in idle:
        @pl.when(flag)
        def _():
            mixed[block(slot)] = jnp.zeros((BLOCK, D), jnp.bfloat16)

    for slot in range(1, 7):
        att[block(slot)] = dot(mixed[block(slot)], w_buf[...], NN).astype(jnp.bfloat16)

    stores = [
        (att.at[own], att_out), (gq.at[own], gq_out), (gk.at[own], gk_out), (gv.at[own], gv_out),
    ]
    for side, near in enumerate((1, 6)):
        stores += [
            (gk.at[block(near)], ret_out.at[side, 0]), (gv.at[block(near)], ret_out.at[side, 1]),
        ]
    outs = [pltpu.make_async_copy(a, b, sem.at[i]) for i, (a, b) in enumerate(stores)]
    for copy in outs:
        copy.start()
    for side, (near, far, shared) in enumerate(((1, 0, l_shared), (6, 7, r_shared))):
        for at, (first_choice, second_choice) in enumerate(((gk, gq), (gv, att))):
            index = len(stores) + 2 * side + at

            @pl.when(shared)
            def _():
                pltpu.make_async_copy(
                    first_choice.at[block(far)], ret_out.at[side, 2 + at], sem.at[index]
                ).start()

            @pl.when(jnp.logical_not(shared))
            def _():
                pltpu.make_async_copy(
                    second_choice.at[block(near)], ret_out.at[side, 2 + at], sem.at[index]
                ).start()

    rows = pl.ds(BLOCK, 6 * BLOCK)

    def weight(i, carry):
        lanes = pl.ds(pl.multiple_of(i * 128, 128), 128)
        gw_buf[lanes] = dot(mixed[rows, lanes], dy_buf[rows], TN).astype(jnp.bfloat16)
        return carry

    lax.fori_loop(0, D // 128, weight, 0)
    gw = pltpu.make_async_copy(gw_buf, gw_out, sem.at[len(loads) - 1])
    gw.start()
    for copy in outs:
        copy.wait()
    for side in range(2):
        for at in range(2):
            index = len(stores) + 2 * side + at
            pltpu.make_async_copy(
                gk.at[block(0)], ret_out.at[side, 2 + at], sem.at[index]
            ).wait()
    gw.wait()


def return_kernel(count, ret_ref, back_ref, send_sem, recv_sem):
    left, right = ring_neighbours(count)
    greet(left, right)
    copies = []
    for side in range(2):
        for slot in range(4):
            copy = pltpu.make_async_remote_copy(
                src_ref=ret_ref.at[side, slot],
                dst_ref=back_ref.at[1 - side, slot],
                send_sem=send_sem.at[side, slot],
                recv_sem=recv_sem.at[1 - side, slot],
                device_id={"tok": right if side else left},
                device_id_type=MESH,
            )
            copy.start()
            copies.append(copy)
    for copy in copies:
        copy.wait()


def settle_kernel(
    flags_ref, back_ref, att_in, gq_in, gk_in, gv_in, att_out, gq_out, gk_out, gv_out, own, extra, sem
):
    def block(i):
        return pl.ds(i * BLOCK, BLOCK)

    for side, (near, far) in enumerate(((0, 1), (3, 2))):
        moved = [
            pltpu.make_async_copy(back_ref.at[side, slot], out.at[block(near)], sem.at[side, slot])
            for slot, out in enumerate((gk_out, gv_out, gq_out, att_out))
        ]
        parts = ((gk_out, near, 0), (gv_out, near, 1), (gk_out, far, 2), (gv_out, far, 3))
        ours = [
            pltpu.make_async_copy(out.at[block(at)], own.at[side, slot], sem.at[side, slot])
            for out, at, slot in parts
        ]
        theirs = [
            pltpu.make_async_copy(
                back_ref.at[side, slot], extra.at[side, slot], sem.at[side, 4 + slot]
            )
            for _, _, slot in parts
        ]
        done = [
            pltpu.make_async_copy(own.at[side, slot], out.at[block(at)], sem.at[side, slot])
            for out, at, slot in parts
        ]

        @pl.when(flags_ref[2 * side] == 1)
        def _():
            for copy in moved:
                copy.start()
            for copy in moved:
                copy.wait()

        @pl.when(flags_ref[2 * side + 1] == 1)
        def _():
            for copy in ours + theirs:
                copy.start()
            for copy in ours + theirs:
                copy.wait()
            for slot in range(4):
                total = own[side, slot].astype(jnp.float32) + extra[side, slot].astype(jnp.float32)
                own[side, slot] = total.astype(jnp.bfloat16)
            for copy in done:
                copy.start()
            for copy in done:
                copy.wait()


def on_device(q_tokens, k_tokens, v_tokens, d_attended, w_out, lengths):
    rows, width = q_tokens.shape[1:]
    count = lax.axis_size("tok")
    norm = 1.0 / math.sqrt(lax.axis_size("dp") * count * rows)
    q, k, v, dy = q_tokens[0], k_tokens[0], v_tokens[0], d_attended[0]
    low = jnp.bfloat16
    vmem, smem, anywhere = (
        pl.BlockSpec(memory_space=space) for space in (pltpu.VMEM, pltpu.SMEM, pl.ANY)
    )
    token_shape = jax.ShapeDtypeStruct((rows, width), low)
    halo_shape = jax.ShapeDtypeStruct((2, 4, BLOCK, width), low)
    big = 58 * 1024 * 1024

    halo, dm = pl.pallas_call(
        functools.partial(exchange_kernel, count),
        out_shape=(halo_shape, token_shape),
        in_specs=[smem] + [vmem] * 5,
        out_specs=(anywhere, vmem),
        scratch_shapes=[
            pltpu.VMEM((2, 2, BLOCK, width), low),
            pltpu.SemaphoreType.DMA((2, 4)),
            pltpu.SemaphoreType.DMA((2, 4)),
        ],
        compiler_params=pltpu.CompilerParams(
            collective_id=0, has_side_effects=True, vmem_limit_bytes=32 * 1024 * 1024
        ),
        name="exchange",
    )(lengths, q, k, v, dy, w_out)

    slab = pltpu.VMEM((SLOTS * BLOCK, width), low)
    att, gq, gk, gv, ret, gw, flags = pl.pallas_call(
        attention_kernel,
        out_shape=(
            token_shape, token_shape, token_shape, token_shape, halo_shape,
            jax.ShapeDtypeStruct((width, width), low),
            jax.ShapeDtypeStruct((4,), jnp.int32),
        ),
        in_specs=[smem] + [anywhere] * 7,
        out_specs=(anywhere,) * 6 + (smem,),
        scratch_shapes=[slab] * 5
        + [pltpu.VMEM((width, width), low)]
        + [slab] * 5
        + [
            pltpu.VMEM((width, width), low),
            pltpu.SMEM((8, 2), jnp.int32),
            pltpu.SemaphoreType.DMA((18,)),
        ],
        compiler_params=pltpu.CompilerParams(vmem_limit_bytes=big),
        name="attention",
    )(lengths, q, k, v, dy, dm, halo, w_out)

    back = pl.pallas_call(
        functools.partial(return_kernel, count),
        out_shape=halo_shape,
        in_specs=[anywhere],
        out_specs=anywhere,
        scratch_shapes=[pltpu.SemaphoreType.DMA((2, 4)), pltpu.SemaphoreType.DMA((2, 4))],
        compiler_params=pltpu.CompilerParams(collective_id=1, has_side_effects=True),
        name="give_back",
    )(ret)

    att, gq, gk, gv = pl.pallas_call(
        settle_kernel,
        out_shape=(token_shape,) * 4,
        in_specs=[smem] + [anywhere] * 5,
        out_specs=(anywhere,) * 4,
        scratch_shapes=[
            pltpu.VMEM((2, 4, BLOCK, width), low),
            pltpu.VMEM((2, 4, BLOCK, width), low),
            pltpu.SemaphoreType.DMA((2, 8)),
        ],
        input_output_aliases={2: 0, 3: 1, 4: 2, 5: 3},
        name="settle",
    )(flags, back, att, gq, gk, gv)

    summed = lax.psum_scatter(gw, "tok", scatter_dimension=0, tiled=True)
    grad_rows = lax.psum(summed, "dp").astype(jnp.float32) * norm
    return (att[None], gq[None], gk[None], gv[None], grad_rows)


def solution(mesh):
    tokens = P("dp", "tok", None)
    return jax.shard_map(
        on_device,
        mesh=mesh,
        in_specs=(tokens, tokens, tokens, tokens, P(), P("dp", None)),
        out_specs=(tokens, tokens, tokens, tokens, P("tok", None)),
        check_vma=False,
    )
```

time: 695 us -> 282 us (0.41)
  the two profiles are of different devices: /device:TPU:0 before, /device:TPU:56 now
where the time goes in v1:
time: 282 us; the launch traced here: 281 us
  Pallas kernels  134 us (48%)
  blocking collectives  87.9 us (31%)
  starting transfers between devices  27.2 us (10%)
  between operations  14.9 us (5%)
  local copies, waits for them, and re-layouts  13.5 us (5%)
    unnamed x1, blocking collectives  87.9 us
    pallas_call x1, Pallas kernels, on_device(): pl.pallas_call(settle_kernel, out_shape=(token_shape,) * 4, in_specs=[sme...  74.5 us
    pallas_call x1, Pallas kernels, on_device(): pl.pallas_call(attention_kernel, out_shape=(token_shape, token_shape, tok...  27.5 us
    unnamed x8, starting transfers between devices  27.1 us
    pallas_call x1, Pallas kernels, on_device(): pl.pallas_call(functools.partial(exchange_kernel, count), out_shape=(halo...  16.3 us
    pallas_call x1, Pallas kernels, on_device(): pl.pallas_call(functools.partial(return_kernel, count), out_shape=halo_sh...  16.2 us
    unnamed x22, local copies, waits for them, and re-layouts  13.5 us
  transfers between devices with their start and end apart: 9, of which 1 were waited for; matrix products, arithmetic and copies ran while one was open for 0% of the time, Pallas kernels for 32%

profile of v1, /device:TPU:56, one launch (start us, length us, event | category | flops | bytes accessed | tf_op | source)
XLA Modules:
  0.0 281.5 jit_solution(951664164365872548)
XLA Ops:
  7.2 0.0 all-reduce.4.cloned.1.call-start
  7.2 0.0 copy-start
  7.2 1.7 copy-done
  9.0 1.3 copy-done.1
  10.2 1.3 copy-done.2
  11.5 1.3 copy-done.3
  12.8 1.3 copy-done.4
  14.0 0.7 copy-done.7
  14.7 16.3 %exchange.1 = (bf16[2,4,128,1152]{3,2,1,0:T(8,128)(2,1)S(1)}, bf16[512,1152]{1,0:T(8,128)(2,1)S(1)}) custom-call(s32[1,64]{1,0:T(1,128)S(1)} %copy-done.7, bf16[512,1152]{1,0:T(8,128)(2,1)S(1)} %bitcast.12, bf16[512,1152]{1,0:T(8,128)(2,1)S(1)} %bitcast.14, bf16[512,1152]{1,0:T(8,128)(2,1)S(1)} %bitcast.16, bf16[512,1152]{1,0:T(8,128)(2,1)S(1)} %bitcast.18, ...), custom_call_target="tpu_custom_call" | custom-call | tf_op jit(solution)/shard_map/exchange/pallas_call | solution.py:368
  31.1 1.4 copy-done.5
  32.5 1.1 copy-done.6
  33.6 27.5 %attention.1 = (bf16[512,1152]{1,0:T(8,128)(2,1)}, bf16[512,1152]{1,0:T(8,128)(2,1)}, bf16[512,1152]{1,0:T(8,128)(2,1)}, bf16[512,1152]{1,0:T(8,128)(2,1)}, bf16...) custom-call(s32[1,64]{1,0:T(1,128)} %lengths_ref.3, bf16[512,1152]{1,0:T(8,128)(2,1)} %bitcast.11, ...), custom_call_target="tpu_custom_call" | custom-call | tf_op jit(solution)/shard_map/attention/pallas_call | solution.py:385
  61.1 0.0 copy-start.8
  61.1 87.9 %fusion = bf16[48,1152]{1,0:T(8,128)(2,1)S(1)} fusion(bf16[1152,1152]{1,0:T(8,128)(2,1)} %get-tuple-element.30), kind=kCustom, calls=%all-reduce-scatter | all-reduce-scatter fusion | flops 1769473 | bytes 2765312
  149.0 1.9 collective-permute-start
  150.9 1.9 collective-permute-start.1
  152.9 1.3 collective-permute-start.7
  154.2 1.3 collective-permute-start.2
  155.5 3.2 %collective-permute-start.3 = (bf16[48,1152]{1,0:T(8,128)(2,1)S(1)}, bf16[48,1152]{1,0:T(8,128)(2,1)S(1)}, u32[]{:S(2)}, u32[]{:S(2)}) collective-permute-start(bf16[48,1152]{1,0:T(8,128)(2,1)S(1)} %fusion), channel_id=1, source_target_pairs={{0,4},{1,5},{2,6},{3,7},{4,8},{5,9},{6,10},{7,11},{8,12},{9,13},{1... | collective-permute-start | bytes 331784
  158.7 12.8 %collective-permute-start.4 = (bf16[48,1152]{1,0:T(8,128)(2,1)S(1)}, bf16[48,1152]{1,0:T(8,128)(2,1)S(1)}, u32[]{:S(2)}, u32[]{:S(2)}) collective-permute-start(bf16[48,1152]{1,0:T(8,128)(2,1)S(1)} %fusion), channel_id=1, source_target_pairs={{0,5},{1,6},{2,7},{3,8},{4,9},{5,10},{6,11},{7,12},{8,13},{9,14},{... | collective-permute-start | bytes 331784
  171.5 0.0 collective-permute-done
  171.5 2.1 collective-permute-start.5
  173.7 2.6 collective-permute-start.6
  176.3 0.6 dynamic-slice.4
  177.5 1.9 collective-permute-done.6
  179.4 2.2 concatenate
  181.7 0.7 constant_dynamic-slice_fusion
  182.3 0.0 all-reduce.4.cloned.1.call-update
  182.3 16.2 %give_back.1.back_ref = bf16[2,4,128,1152]{3,2,1,0:T(8,128)(2,1)} custom-call(bf16[2,4,128,1152]{3,2,1,0:T(8,128)(2,1)} %get-tuple-element.21.ret_ref), custom_call_target="tpu_custom_call" | custom-call | tf_op jit(solution)/shard_map/give_back/pallas_call | solution.py:406
  198.5 74.5 %settle.1 = (bf16[512,1152]{1,0:T(8,128)(2,1)}, bf16[512,1152]{1,0:T(8,128)(2,1)}, bf16[512,1152]{1,0:T(8,128)(2,1)}, bf16[512,1152]{1,0:T(8,128)(2,1)}) custom-call(s32[4]{0:T(128)} %get-tuple-element.20.flags_ref, bf16[2,4,128,1152]{3,2,1,0:T(8,128)(2,1)} %give_back.1.back_ref, ...), custom_call_target="tpu_custom_call", output_to_operand_aliasing={{0}: (2, {}), {1}: (3, {}), {2}: (4, {}), {3}: (5, {})} | custom-call | tf_op jit(solution)/shard_map/settle/pallas_call | solution.py:416
  273.0 0.0 all-reduce.4.cloned.1.call-done
  273.0 1.6 convert_multiply_fusion
  (15 shorter events, 0.1 us)
Async XLA Ops:
  7.2 265.9 %all-reduce.4.cloned.1.call-start = ((), (), s32[]{:S(2)}) async-start(), calls=%async_computation | async-start | bytes 184320 | tf_op jit(solution)/shard_map/psum | solution.py:431
  7.2 1.8 copy-start
  9.0 1.3 copy-start.1
  10.2 1.3 copy-start.2
  11.5 1.3 copy-start.3
  12.8 1.3 copy-start.4
  14.0 0.7 copy-start.7
  31.0 1.5 copy-start.5
  32.5 1.1 copy-start.6
  61.1 115.2 %copy-start.8 = (u32[128]{0:T(128)S(1)}, u32[128]{0:T(128)}, u32[]{:S(2)}) copy-start(u32[128]{0:T(128)} %constant.9) | copy-start | bytes 1540
  149.0 22.5 %collective-permute-start = (bf16[48,1152]{1,0:T(8,128)(2,1)S(1)}, bf16[48,1152]{1,0:T(8,128)(2,1)S(1)}, u32[]{:S(2)}, u32[]{:S(2)}) collective-permute-start(bf16[48,1152]{1,0:T(8,128)(2,1)S(1)} %fusion), channel_id=1, source_target_pairs={{0,1},{1,2},{2,3},{3,4},{4,5},{5,6},{6,7},{7,8},{8,9},{9,10},{10,1... | collective-permute-start | bytes 331784
  150.9 22.7 %collective-permute-start.1 = (bf16[48,1152]{1,0:T(8,128)(2,1)S(1)}, bf16[48,1152]{1,0:T(8,128)(2,1)S(1)}, u32[]{:S(2)}, u32[]{:S(2)}) collective-permute-start(bf16[48,1152]{1,0:T(8,128)(2,1)S(1)} %fusion), channel_id=1, source_target_pairs={{0,2},{1,3},{2,4},{3,5},{4,6},{5,7},{6,8},{7,9},{8,10},{9,11},{10,... | collective-permute-start | bytes 331784
  152.9 5.8 %collective-permute-start.7 = (bf16[36,1152]{1,0:T(8,128)(2,1)S(1)}, bf16[36,1152]{1,0:T(8,128)(2,1)S(1)}, u32[]{:S(2)}, u32[]{:S(2)}) collective-permute-start(bf16[36,1152]{1,0:T(8,128)(2,1)S(1)} %slice), channel_id=1, source_target_pairs={{0,8},{1,9},{2,10},{3,11},{4,12},{5,13},{6,14},{7,15},{8,16},{9,17... | collective-permute-start | bytes 248840
  154.2 23.3 %collective-permute-start.2 = (bf16[48,1152]{1,0:T(8,128)(2,1)S(1)}, bf16[48,1152]{1,0:T(8,128)(2,1)S(1)}, u32[]{:S(2)}, u32[]{:S(2)}) collective-permute-start(bf16[48,1152]{1,0:T(8,128)(2,1)S(1)} %fusion), channel_id=1, source_target_pairs={{0,3},{1,4},{2,5},{3,6},{4,7},{5,8},{6,9},{7,10},{8,11},{9,12},{10... | collective-permute-start | bytes 331784
  155.5 22.0 %collective-permute-start.3 = (bf16[48,1152]{1,0:T(8,128)(2,1)S(1)}, bf16[48,1152]{1,0:T(8,128)(2,1)S(1)}, u32[]{:S(2)}, u32[]{:S(2)}) collective-permute-start(bf16[48,1152]{1,0:T(8,128)(2,1)S(1)} %fusion), channel_id=1, source_target_pairs={{0,4},{1,5},{2,6},{3,7},{4,8},{5,9},{6,10},{7,11},{8,12},{9,13},{1... | collective-permute-start | bytes 331784
  158.7 18.8 %collective-permute-start.4 = (bf16[48,1152]{1,0:T(8,128)(2,1)S(1)}, bf16[48,1152]{1,0:T(8,128)(2,1)S(1)}, u32[]{:S(2)}, u32[]{:S(2)}) collective-permute-start(bf16[48,1152]{1,0:T(8,128)(2,1)S(1)} %fusion), channel_id=1, source_target_pairs={{0,5},{1,6},{2,7},{3,8},{4,9},{5,10},{6,11},{7,12},{8,13},{9,14},{... | collective-permute-start | bytes 331784
  171.5 6.0 %collective-permute-start.5 = (bf16[48,1152]{1,0:T(8,128)(2,1)S(1)}, bf16[48,1152]{1,0:T(8,128)(2,1)S(1)}, u32[]{:S(2)}, u32[]{:S(2)}) collective-permute-start(bf16[48,1152]{1,0:T(8,128)(2,1)S(1)} %fusion), channel_id=1, source_target_pairs={{0,6},{1,7},{2,8},{3,9},{4,10},{5,11},{6,12},{7,13},{8,14},{9,15},... | collective-permute-start | bytes 331784
  173.7 5.8 %collective-permute-start.6 = (bf16[48,1152]{1,0:T(8,128)(2,1)S(1)}, bf16[48,1152]{1,0:T(8,128)(2,1)S(1)}, u32[]{:S(2)}, u32[]{:S(2)}) collective-permute-start(bf16[48,1152]{1,0:T(8,128)(2,1)S(1)} %fusion), channel_id=1, source_target_pairs={{0,7},{1,8},{2,9},{3,10},{4,11},{5,12},{6,13},{7,14},{8,15},{9,16}... | collective-permute-start | bytes 331784
Sparse Core Ops, SparseCore 0:
  182.5 38.8 all-reduce.3

commit v2 on v1

--- a/solution.py
+++ b/solution.py
@@ -17,6 +17,9 @@
 WINDOW = 256
 SCALE = HEAD_DIM ** (-0.5)
 EXP2_SCALE = SCALE * math.log2(math.e)
+PART = 36
+PAD = 48
+SIDE = 4
 MESH = pl.DeviceIdType.MESH
 NN = (((1,), (0,)), ((), ()))
 NT = (((1,), (1,)), ((), ()))
@@ -39,11 +42,12 @@
     return before, after
 
 
-def greet(left, right):
+def greet(others):
     barrier = pltpu.get_barrier_semaphore()
-    for other in (left, right):
-        pl.semaphore_signal(barrier, inc=1, device_id={"tok": other}, device_id_type=MESH)
-    pl.semaphore_wait(barrier, 2)
+    for other in others:
+        where = other if isinstance(other, dict) else {"tok": other}
+        pl.semaphore_signal(barrier, inc=1, device_id=where, device_id_type=MESH)
+    pl.semaphore_wait(barrier, len(others))
 
 
 def ring_neighbours(count):
@@ -52,11 +56,25 @@
 
 
 def exchange_kernel(
-    count, lengths_ref, q_ref, k_ref, v_ref, dy_ref, w_ref, halo_ref, dm_ref, pack, send_sem, recv_sem
+    count, lengths_ref, q_ref, k_ref, v_ref, dy_ref, w_ref, halo_ref, dm_ref,
+    dy_buf, w_buf, near_buf, far_buf, pack, load_sem, send_sem, recv_sem,
 ):
     left, right = ring_neighbours(count)
     first = lax.axis_index("tok") * OWN
-    greet(left, right)
+    near = [pl.ds(0, BLOCK), pl.ds(3 * BLOCK, BLOCK)]
+    far = [pl.ds(BLOCK, BLOCK), pl.ds(2 * BLOCK, BLOCK)]
+    loads = []
+    for side in range(2):
+        loads += [
+            (q_ref.at[near[side]], near_buf.at[side]),
+            (k_ref.at[far[side]], far_buf.at[side, 0]),
+            (v_ref.at[far[side]], far_buf.at[side, 1]),
+        ]
+    loads += [(dy_ref, dy_buf), (w_ref, w_buf)]
+    loads = [pltpu.make_async_copy(a, b, load_sem.at[i]) for i, (a, b) in enumerate(loads)]
+    for load in loads:
+        load.start()
+    greet((left, right))
     copies = []
 
     def send(side, slot, source):
@@ -71,21 +89,22 @@
         copy.start()
         copies.append(copy)
 
-    near = [slice(0, BLOCK), slice(3 * BLOCK, 4 * BLOCK)]
-    far = [slice(BLOCK, 2 * BLOCK), slice(2 * BLOCK, 3 * BLOCK)]
     for side in range(2):
         send(side, 0, k_ref.at[near[side]])
         send(side, 1, v_ref.at[near[side]])
+    for load in loads[:-1]:
+        load.wait()
     for side in range(2):
         before, after = boundary(lengths_ref, first + side * OWN)
         shared = jnp.logical_and(before == 2, after == 2)
-        pack[side, 0] = jnp.where(shared, k_ref[far[side]], q_ref[near[side]])
-        pack[side, 1] = jnp.where(shared, v_ref[far[side]], dy_ref[near[side]])
+        pack[side, 0] = jnp.where(shared, far_buf[side, 0], near_buf[side])
+        pack[side, 1] = jnp.where(shared, far_buf[side, 1], dy_buf[near[side]])
         send(side, 2, pack.at[side, 0])
         send(side, 3, pack.at[side, 1])
+    loads[-1].wait()
     for part in range(OWN):
         rows = slice(part * BLOCK, (part + 1) * BLOCK)
-        dm_ref[rows] = dot(dy_ref[rows], w_ref[...], NT).astype(jnp.bfloat16)
+        dm_ref[rows] = dot(dy_buf[rows], w_buf[...], NT).astype(jnp.bfloat16)
     for copy in copies:
         copy.wait()
 
@@ -136,7 +155,7 @@
 def attention_kernel(
     lengths_ref, q_ref, k_ref, v_ref, dy_ref, dm_ref, halo_ref, w_ref,
     att_out, gq_out, gk_out, gv_out, ret_out, gw_out, flags_out,
-    q_buf, k_buf, v_buf, dy_buf, dm_buf, w_buf, mixed, gq, gk, gv, att, gw_buf, work, sem,
+    q_buf, k_buf, v_buf, dy_buf, dm_buf, w_buf, mixed, gq, gk, gv, att, gw_buf, gw_parts, work, sem,
 ):
     first = lax.axis_index("tok") * OWN
     last = first + OWN
@@ -266,11 +285,17 @@
 
     def weight(i, carry):
         lanes = pl.ds(pl.multiple_of(i * 128, 128), 128)
-        gw_buf[lanes] = dot(mixed[rows, lanes], dy_buf[rows], TN).astype(jnp.bfloat16)
+        gw_buf[lanes] = dot(mixed[rows, lanes], dy_buf[rows], TN)
         return carry
 
     lax.fori_loop(0, D // 128, weight, 0)
-    gw = pltpu.make_async_copy(gw_buf, gw_out, sem.at[len(loads) - 1])
+    gw_buf[D:] = jnp.zeros((PAD - PART, D), jnp.float32)
+    for part in range(D // PART):
+        x, z, core = part // 8, part // 2 % 4, part % 2
+        place = (z, x) if core else (x, z)
+        chunk = gw_buf[part * PART : part * PART + PAD]
+        gw_parts[core, place[0], place[1]] = chunk.astype(jnp.bfloat16)
+    gw = pltpu.make_async_copy(gw_parts, gw_out, sem.at[len(loads) - 1])
     gw.start()
     for copy in outs:
         copy.wait()
@@ -283,37 +308,161 @@
     gw.wait()
 
 
-def return_kernel(count, ret_ref, back_ref, send_sem, recv_sem):
+def finish_kernel(
+    count, ret_ref, gw_ref, back_ref, sum_ref,
+    mine, sibling, total, second, third, fourth, fifth,
+    ret_send, ret_recv, load_sem, one_send, one_recv, sends, recvs,
+):
     left, right = ring_neighbours(count)
-    greet(left, right)
+    me, y = lax.axis_index("tok"), lax.axis_index("dp")
+    core, z, x = lax.rem(me, 2), lax.rem(me // 2, SIDE), me // (2 * SIDE)
+    own = pltpu.make_async_copy(gw_ref.at[core], mine, load_sem)
+    own.start()
+
+    def device(x, y, z, core):
+        return {"dp": y, "tok": (x * SIDE + z) * 2 + core}
+
+    def turned(at, step):
+        return lax.rem(at + step, SIDE)
+
+    other = device(x, y, z, 1 - core)
+    steps = range(1, SIDE)
+    along_x = [device(turned(x, step), y, z, core) for step in steps]
+    along_y = [device(x, turned(y, step), z, core) for step in steps]
+    along_z = [device(x, y, turned(z, step), core) for step in steps]
+    greet([left, right, other] + along_x + along_y + along_z)
+
+    one = []
+    for row in range(SIDE):
+        copy = pltpu.make_async_remote_copy(
+            src_ref=gw_ref.at[1 - core, row],
+            dst_ref=sibling.at[row],
+            send_sem=one_send.at[row],
+            recv_sem=one_recv.at[row],
+            device_id=other,
+            device_id_type=MESH,
+        )
+        copy.start()
+        one.append(copy)
     copies = []
     for side in range(2):
         for slot in range(4):
             copy = pltpu.make_async_remote_copy(
                 src_ref=ret_ref.at[side, slot],
                 dst_ref=back_ref.at[1 - side, slot],
-                send_sem=send_sem.at[side, slot],
-                recv_sem=recv_sem.at[1 - side, slot],
+                send_sem=ret_send.at[side, slot],
+                recv_sem=ret_recv.at[1 - side, slot],
                 device_id={"tok": right if side else left},
                 device_id_type=MESH,
             )
             copy.start()
             copies.append(copy)
+
+    own.wait()
+    for row in range(SIDE):
+        one[row].wait()
+        for column in range(SIDE):
+            both = mine[row, column].astype(jnp.float32) + sibling[row, column].astype(jnp.float32)
+            total[row, column] = both.astype(jnp.bfloat16)
+
+    def spread(stage, source, landing, first_axis):
+        at = jnp.where(first_axis, x, y)
+        started = []
+        for step in steps:
+            there = turned(at, step)
+            where = device(
+                jnp.where(first_axis, there, x), jnp.where(first_axis, y, there), z, core
+            )
+            copy = pltpu.make_async_remote_copy(
+                src_ref=source.at[there],
+                dst_ref=landing.at[step - 1],
+                send_sem=sends.at[stage, step - 1],
+                recv_sem=recvs.at[stage, step - 1],
+                device_id=where,
+                device_id_type=MESH,
+            )
+            copy.start()
+            started.append(copy)
+        return at, started
+
+    at, started = spread(0, total, second, core == 0)
+    for copy in started:
+        copy.wait()
+    for column in range(SIDE):
+        whole = total[at, column].astype(jnp.float32)
+        for step in range(SIDE - 1):
+            whole = whole + second[step, column].astype(jnp.float32)
+        mine[0, column] = whole.astype(jnp.bfloat16)
+    at, started = spread(1, mine.at[0], third, core == 1)
+    for copy in started:
+        copy.wait()
+    whole = mine[0, at].astype(jnp.float32)
+    for step in range(SIDE - 1):
+        whole = whole + third[step].astype(jnp.float32)
+    sum_ref[...] = whole.astype(jnp.bfloat16)
+
+    gap = lax.rem(z - y + SIDE, SIDE)
+
+    def to_plane(step):
+        return pltpu.make_async_remote_copy(
+            src_ref=sum_ref,
+            dst_ref=fourth.at[step - 1],
+            send_sem=sends.at[2, step - 1],
+            recv_sem=recvs.at[2, step - 1],
+            device_id=device(x, y, turned(z, SIDE - step), core),
+            device_id_type=MESH,
+        )
+
+    def to_row(step):
+        return pltpu.make_async_remote_copy(
+            src_ref=fifth.at[0],
+            dst_ref=fifth.at[1],
+            send_sem=sends.at[3, step - 1],
+            recv_sem=recvs.at[3, 0],
+            device_id=device(x, turned(y, step), z, core),
+            device_id_type=MESH,
+        )
+
+    for step in steps:
+        @pl.when(gap == step)
+        def _():
+            copy = to_plane(step)
+            copy.start()
+            copy.wait_send()
+
+    @pl.when(gap == 0)
+    def _():
+        for step in steps:
+            to_plane(step).wait_recv()
+        whole = sum_ref[...].astype(jnp.float32)
+        for step in range(SIDE - 1):
+            whole = whole + fourth[step].astype(jnp.float32)
+        fifth[0] = whole.astype(jnp.bfloat16)
+        started = [to_row(step) for step in steps]
+        for copy in started:
+            copy.start()
+        for copy in started:
+            copy.wait_send()
+        sum_ref[...] = fifth[0]
+
+    @pl.when(gap != 0)
+    def _():
+        to_row(1).wait_recv()
+        sum_ref[...] = fifth[1]
+
     for copy in copies:
         copy.wait()
 
 
 def settle_kernel(
-    flags_ref, back_ref, att_in, gq_in, gk_in, gv_in, att_out, gq_out, gk_out, gv_out, own, extra, sem
+    norm, flags_ref, sum_ref, back_ref, att_in, gq_in, gk_in, gv_in,
+    att_out, gq_out, gk_out, gv_out, rows_ref, own, extra, sem,
 ):
     def block(i):
         return pl.ds(i * BLOCK, BLOCK)
 
+    rows_ref[...] = sum_ref[:PART].astype(jnp.float32) * norm
     for side, (near, far) in enumerate(((0, 1), (3, 2))):
-        moved = [
-            pltpu.make_async_copy(back_ref.at[side, slot], out.at[block(near)], sem.at[side, slot])
-            for slot, out in enumerate((gk_out, gv_out, gq_out, att_out))
-        ]
         parts = ((gk_out, near, 0), (gv_out, near, 1), (gk_out, far, 2), (gv_out, far, 3))
         ours = [
             pltpu.make_async_copy(out.at[block(at)], own.at[side, slot], sem.at[side, slot])
@@ -323,15 +472,23 @@
             pltpu.make_async_copy(
                 back_ref.at[side, slot], extra.at[side, slot], sem.at[side, 4 + slot]
             )
-            for _, _, slot in parts
+            for slot in range(4)
         ]
-        done = [
+        moved = [
+            pltpu.make_async_copy(extra.at[side, slot], out.at[block(near)], sem.at[side, slot])
+            for slot, out in enumerate((gk_out, gv_out, gq_out, att_out))
+        ]
+        added = [
             pltpu.make_async_copy(own.at[side, slot], out.at[block(at)], sem.at[side, slot])
             for out, at, slot in parts
         ]
 
         @pl.when(flags_ref[2 * side] == 1)
         def _():
+            for copy in theirs:
+                copy.start()
+            for copy in theirs:
+                copy.wait()
             for copy in moved:
                 copy.start()
             for copy in moved:
@@ -344,11 +501,11 @@
             for copy in ours + theirs:
                 copy.wait()
             for slot in range(4):
-                total = own[side, slot].astype(jnp.float32) + extra[side, slot].astype(jnp.float32)
-                own[side, slot] = total.astype(jnp.bfloat16)
-            for copy in done:
+                both = own[side, slot].astype(jnp.float32) + extra[side, slot].astype(jnp.float32)
+                own[side, slot] = both.astype(jnp.bfloat16)
+            for copy in added:
                 copy.start()
-            for copy in done:
+            for copy in added:
                 copy.wait()
 
 
@@ -363,20 +520,26 @@
     )
     token_shape = jax.ShapeDtypeStruct((rows, width), low)
     halo_shape = jax.ShapeDtypeStruct((2, 4, BLOCK, width), low)
+    parts_shape = jax.ShapeDtypeStruct((2, SIDE, SIDE, PAD, width), low)
     big = 58 * 1024 * 1024
 
     halo, dm = pl.pallas_call(
         functools.partial(exchange_kernel, count),
         out_shape=(halo_shape, token_shape),
-        in_specs=[smem] + [vmem] * 5,
+        in_specs=[smem] + [anywhere] * 5,
         out_specs=(anywhere, vmem),
         scratch_shapes=[
+            pltpu.VMEM((rows, width), low),
+            pltpu.VMEM((width, width), low),
+            pltpu.VMEM((2, BLOCK, width), low),
             pltpu.VMEM((2, 2, BLOCK, width), low),
+            pltpu.VMEM((2, 2, BLOCK, width), low),
+            pltpu.SemaphoreType.DMA((8,)),
             pltpu.SemaphoreType.DMA((2, 4)),
             pltpu.SemaphoreType.DMA((2, 4)),
         ],
         compiler_params=pltpu.CompilerParams(
-            collective_id=0, has_side_effects=True, vmem_limit_bytes=32 * 1024 * 1024
+            collective_id=0, has_side_effects=True, vmem_limit_bytes=big
         ),
         name="exchange",
     )(lengths, q, k, v, dy, w_out)
@@ -386,7 +549,7 @@
         attention_kernel,
         out_shape=(
             token_shape, token_shape, token_shape, token_shape, halo_shape,
-            jax.ShapeDtypeStruct((width, width), low),
+            parts_shape,
             jax.ShapeDtypeStruct((4,), jnp.int32),
         ),
         in_specs=[smem] + [anywhere] * 7,
@@ -395,7 +558,8 @@
         + [pltpu.VMEM((width, width), low)]
         + [slab] * 5
         + [
-            pltpu.VMEM((width, width), low),
+            pltpu.VMEM((width + PAD - PART, width), jnp.float32),
+            pltpu.VMEM(parts_shape.shape, low),
             pltpu.SMEM((8, 2), jnp.int32),
             pltpu.SemaphoreType.DMA((18,)),
         ],
@@ -403,32 +567,42 @@
         name="attention",
     )(lengths, q, k, v, dy, dm, halo, w_out)
 
-    back = pl.pallas_call(
-        functools.partial(return_kernel, count),
-        out_shape=halo_shape,
-        in_specs=[anywhere],
-        out_specs=anywhere,
-        scratch_shapes=[pltpu.SemaphoreType.DMA((2, 4)), pltpu.SemaphoreType.DMA((2, 4))],
-        compiler_params=pltpu.CompilerParams(collective_id=1, has_side_effects=True),
-        name="give_back",
-    )(ret)
-
-    att, gq, gk, gv = pl.pallas_call(
-        settle_kernel,
-        out_shape=(token_shape,) * 4,
-        in_specs=[smem] + [anywhere] * 5,
-        out_specs=(anywhere,) * 4,
+    piece = pltpu.VMEM((SIDE - 1, PAD, width), low)
+    quarter = pltpu.VMEM((SIDE, SIDE, PAD, width), low)
+    dma = pltpu.SemaphoreType.DMA
+    back, summed = pl.pallas_call(
+        functools.partial(finish_kernel, count),
+        out_shape=(halo_shape, jax.ShapeDtypeStruct((PAD, width), low)),
+        in_specs=[anywhere] * 2,
+        out_specs=(anywhere, vmem),
+        scratch_shapes=[
+            quarter, quarter, quarter,
+            pltpu.VMEM((SIDE - 1, SIDE, PAD, width), low),
+            piece, piece,
+            pltpu.VMEM((2, PAD, width), low),
+            dma((2, 4)), dma((2, 4)), dma, dma((SIDE,)), dma((SIDE,)),
+            dma((4, SIDE - 1)), dma((4, SIDE - 1)),
+        ],
+        compiler_params=pltpu.CompilerParams(
+            collective_id=1, has_side_effects=True, vmem_limit_bytes=big
+        ),
+        name="finish",
+    )(ret, gw)
+
+    att, gq, gk, gv, grad_rows = pl.pallas_call(
+        functools.partial(settle_kernel, norm),
+        out_shape=(token_shape,) * 4 + (jax.ShapeDtypeStruct((PART, width), jnp.float32),),
+        in_specs=[smem, vmem] + [anywhere] * 5,
+        out_specs=(anywhere,) * 4 + (vmem,),
         scratch_shapes=[
             pltpu.VMEM((2, 4, BLOCK, width), low),
             pltpu.VMEM((2, 4, BLOCK, width), low),
-            pltpu.SemaphoreType.DMA((2, 8)),
+            dma((2, 8)),
         ],
-        input_output_aliases={2: 0, 3: 1, 4: 2, 5: 3},
+        input_output_aliases={3: 0, 4: 1, 5: 2, 6: 3},
+        compiler_params=pltpu.CompilerParams(vmem_limit_bytes=big),
         name="settle",
-    )(flags, back, att, gq, gk, gv)
-
-    summed = lax.psum_scatter(gw, "tok", scatter_dimension=0, tiled=True)
-    grad_rows = lax.psum(summed, "dp").astype(jnp.float32) * norm
+    )(flags, summed, back, att, gq, gk, gv)
     return (att[None], gq[None], gk[None], gv[None], grad_rows)
 
 

time: 282 us -> 121 us (0.43)
  the two profiles are of different devices: /device:TPU:56 before, /device:TPU:64 now
where the time goes in v2:
time: 121 us
  Pallas kernels  120 us (99%)
    pallas_call x1, Pallas kernels, on_device(): pl.pallas_call(functools.partial(finish_kernel, count), out_shape=(halo_s...  67.8 us
    pallas_call x1, Pallas kernels, on_device(): pl.pallas_call(attention_kernel, out_shape=(token_shape, token_shape, tok...  30.3 us
    pallas_call x1, Pallas kernels, on_device(): pl.pallas_call(functools.partial(exchange_kernel, count), out_shape=(halo...  18 us
    pallas_call x1, Pallas kernels, on_device(): pl.pallas_call(functools.partial(settle_kernel, norm), out_shape=(token_s...  3.96 us

profile of v2, /device:TPU:64, one launch (start us, length us, event | category | flops | bytes accessed | tf_op | source)
XLA Modules:
  0.0 120.9 jit_solution(15610326071685111856)
XLA Ops:
  0.6 18.0 %exchange.1 = (bf16[2,4,128,1152]{3,2,1,0:T(8,128)(2,1)}, bf16[512,1152]{1,0:T(8,128)(2,1)}) custom-call(s32[1,64]{1,0:T(1,128)} %lengths_ref.3, bf16[512,1152]{1,0:T(8,128)(2,1)} %bitcast.8, bf16[512,1152]{1,0:T(8,128)(2,1)} %bitcast.10, bf16[512,1152]{1,0:T(8,128)(2,1)} %bitcast.12, bf16[512,1152]{1,0:T(8,128)(2,1)} %bitcast.14, bf16[1152,1152]{1,0:T(8,128)(2,1)} %w_ref.3), custom_call_target="tpu_custom_call" | custom-call | tf_op jit(solution)/shard_map/exchange/pallas_call | solution.py:526
  18.7 30.3 %attention.1 = (bf16[512,1152]{1,0:T(8,128)(2,1)}, bf16[512,1152]{1,0:T(8,128)(2,1)}, bf16[512,1152]{1,0:T(8,128)(2,1)}, bf16[512,1152]{1,0:T(8,128)(2,1)}, bf16...) custom-call(s32[1,64]{1,0:T(1,128)} %lengths_ref.3, bf16[512,1152]{1,0:T(8,128)(2,1)} %bitcast.9, ...), custom_call_target="tpu_custom_call" | custom-call | tf_op jit(solution)/shard_map/attention/pallas_call | solution.py:548
  48.9 67.8 %finish.1 = (bf16[2,4,128,1152]{3,2,1,0:T(8,128)(2,1)}, bf16[48,1152]{1,0:T(8,128)(2,1)}) custom-call(bf16[2,4,128,1152]{3,2,1,0:T(8,128)(2,1)} %get-tuple-element.24.ret_ref, bf16[2,4,4,48,1152]{4,3,2,1,0:T(8,128)(2,1)} %get-tuple-element.25.gw_ref), custom_call_target="tpu_custom_call" | custom-call | tf_op jit(solution)/shard_map/finish/pallas_call | solution.py:573
  116.7 4.0 %settle.1 = (bf16[512,1152]{1,0:T(8,128)(2,1)}, bf16[512,1152]{1,0:T(8,128)(2,1)}, bf16[512,1152]{1,0:T(8,128)(2,1)}, bf16[512,1152]{1,0:T(8,128)(2,1)}, f32[36,1152]{1,0:T(8,128)}) custom-call(s32[4]{0:T(128)} %get-tuple-element.23.flags_ref, ...), custom_call_target="tpu_custom_call", output_to_operand_aliasing={{0}: (3, {}), {1}: (4, {}), {2}: (5, {}), {3}: (6, {})} | custom-call | tf_op jit(solution)/shard_map/settle/pallas_call | solution.py:592

commit v3 on v2

v3 whole, which is shorter than its diff:
```python
import functools
import math

import jax
import jax.numpy as jnp
from jax import lax
from jax.experimental import pallas as pl
from jax.experimental.pallas import tpu as pltpu
from jax.sharding import PartitionSpec as P

HEADS = 16
HEAD_DIM = 72
BLOCK = 128
D = 1152
OWN = 4
SLOTS = 8
WINDOW = 256
SCALE = HEAD_DIM ** (-0.5)
EXP2_SCALE = SCALE * math.log2(math.e)
PART = 36
PIECE = 384
PIECES = D // PIECE
PACKED = 112
SIDE = 4
MESH = pl.DeviceIdType.MESH
NN = (((1,), (0,)), ((), ()))
NT = (((1,), (1,)), ((), ()))
TN = (((0,), (0,)), ((), ()))


def dot(a, b, dims):
    return lax.dot_general(a, b, dims, preferred_element_type=jnp.float32)


def boundary(lengths_ref, edge):
    def step(i, carry):
        start, before, after = carry
        end = start + lengths_ref[0, i]
        hit = jnp.logical_and(start < edge, end > edge)
        return (end, jnp.where(hit, edge - start, before), jnp.where(hit, end - edge, after))

    zero = jnp.int32(0)
    _, before, after = lax.fori_loop(0, lengths_ref.shape[1], step, (zero, zero, zero))
    return before, after


def greet(others):
    barrier = pltpu.get_barrier_semaphore()
    for other in others:
        where = other if isinstance(other, dict) else {"tok": other}
        pl.semaphore_signal(barrier, inc=1, device_id=where, device_id_type=MESH)
    pl.semaphore_wait(barrier, len(others))


def ring_neighbours(count):
    me = lax.axis_index("tok")
    return lax.rem(me + count - 1, count), lax.rem(me + 1, count)


def exchange_kernel(
    count, lengths_ref, q_ref, k_ref, v_ref, dy_ref, w_ref, halo_ref, dm_ref,
    dy_buf, w_buf, near_buf, far_buf, pack, load_sem, send_sem, recv_sem,
):
    left, right = ring_neighbours(count)
    first = lax.axis_index("tok") * OWN
    near = [pl.ds(0, BLOCK), pl.ds(3 * BLOCK, BLOCK)]
    far = [pl.ds(BLOCK, BLOCK), pl.ds(2 * BLOCK, BLOCK)]
    loads = []
    for side in range(2):
        loads += [
            (q_ref.at[near[side]], near_buf.at[side]),
            (k_ref.at[far[side]], far_buf.at[side, 0]),
            (v_ref.at[far[side]], far_buf.at[side, 1]),
        ]
    loads += [(dy_ref, dy_buf), (w_ref, w_buf)]
    loads = [pltpu.make_async_copy(a, b, load_sem.at[i]) for i, (a, b) in enumerate(loads)]
    for load in loads:
        load.start()
    greet((left, right))
    copies = []

    def send(side, slot, source):
        copy = pltpu.make_async_remote_copy(
            src_ref=source,
            dst_ref=halo_ref.at[1 - side, slot],
            send_sem=send_sem.at[side, slot],
            recv_sem=recv_sem.at[1 - side, slot],
            device_id={"tok": right if side else left},
            device_id_type=MESH,
        )
        copy.start()
        copies.append(copy)

    for side in range(2):
        send(side, 0, k_ref.at[near[side]])
        send(side, 1, v_ref.at[near[side]])
    for load in loads[:-1]:
        load.wait()
    for side in range(2):
        before, after = boundary(lengths_ref, first + side * OWN)
        shared = jnp.logical_and(before == 2, after == 2)
        pack[side, 0] = jnp.where(shared, far_buf[side, 0], near_buf[side])
        pack[side, 1] = jnp.where(shared, far_buf[side, 1], dy_buf[near[side]])
        send(side, 2, pack.at[side, 0])
        send(side, 3, pack.at[side, 1])
    loads[-1].wait()
    for part in range(OWN):
        rows = slice(part * BLOCK, (part + 1) * BLOCK)
        dm_ref[rows] = dot(dy_buf[rows], w_buf[...], NT).astype(jnp.bfloat16)
    for copy in copies:
        copy.wait()


def attend(q_buf, k_buf, v_buf, dm_buf, mixed, gq, gk, gv, q_at, q_blocks, k_at, k_blocks):
    q_rows = pl.ds(pl.multiple_of(q_at * BLOCK, BLOCK), q_blocks * BLOCK)
    k_rows = pl.ds(pl.multiple_of(k_at * BLOCK, BLOCK), k_blocks * BLOCK)
    lane = lax.broadcasted_iota(jnp.int32, (1, WINDOW), 1)

    group = {1: 8, 2: 4, 3: 2, 4: 2}[k_blocks]

    def several(i, carry):
        heads = []
        for j in range(group):
            at = (group * i + j) * HEAD_DIM
            base = jnp.minimum(at // 128, (D - WINDOW) // 128) * 128
            offset = at - base
            window = pl.ds(pl.multiple_of(base, 128), WINDOW)
            inside = jnp.logical_and(lane >= offset, lane < offset + HEAD_DIM)
            keep = jnp.where(inside, 1.0, 0.0).astype(jnp.bfloat16)
            heads.append((offset, window, keep))
        probs_of, ds_of = [], []
        for offset, window, keep in heads:
            scores = dot(k_buf[k_rows, window] * keep, q_buf[q_rows, window], NT)
            d_probs = dot(v_buf[k_rows, window] * keep, dm_buf[q_rows, window], NT)
            top = jnp.max(scores, axis=0, keepdims=True)
            weights = jnp.exp2((scores - top) * EXP2_SCALE)
            probs = weights * (1.0 / jnp.sum(weights, axis=0, keepdims=True))
            product = probs * d_probs
            delta = jnp.sum(product, axis=0, keepdims=True)
            probs_of.append(probs.astype(jnp.bfloat16))
            ds_of.append((product - probs * delta).astype(jnp.bfloat16))
        news = []
        for (offset, window, keep), p, ds in zip(heads, probs_of, ds_of):
            news.append((
                dot(p, v_buf[k_rows, window], TN), dot(p, dm_buf[q_rows, window], NN),
                dot(ds, k_buf[k_rows, window], TN) * SCALE, dot(ds, q_buf[q_rows, window], NN) * SCALE,
            ))
        for (offset, window, keep), new in zip(heads, news):
            for ref, rows, value in zip((mixed, gv, gq, gk), (q_rows, k_rows, q_rows, k_rows), new):
                old = ref[rows, window]
                ref[rows, window] = jnp.where(lane < offset, old, value.astype(jnp.bfloat16))
        return carry

    lax.fori_loop(0, HEADS // group, several, 0)


def attention_kernel(
    lengths_ref, q_ref, k_ref, v_ref, dm_ref, halo_ref, w_ref,
    mixed_out, gq_out, gk_out, gv_out, ret_out, flags_out,
    q_buf, k_buf, v_buf, dm_buf, w_buf, dy_buf, mixed, gq, gk, gv, att, work, sem,
):
    first = lax.axis_index("tok") * OWN
    last = first + OWN
    own = pl.ds(2 * BLOCK, OWN * BLOCK)

    def block(i):
        return pl.ds(i * BLOCK, BLOCK)

    loads = [
        (q_ref, q_buf.at[own]), (k_ref, k_buf.at[own]), (v_ref, v_buf.at[own]),
        (dm_ref, dm_buf.at[own]), (w_ref, w_buf),
    ]
    for side, (near, far) in enumerate(((1, 0), (6, 7))):
        loads += [
            (halo_ref.at[side, 0], k_buf.at[block(near)]),
            (halo_ref.at[side, 1], v_buf.at[block(near)]),
            (halo_ref.at[side, 2], q_buf.at[block(near)]),
            (halo_ref.at[side, 2], k_buf.at[block(far)]),
            (halo_ref.at[side, 3], dy_buf.at[side]),
            (halo_ref.at[side, 3], v_buf.at[block(far)]),
        ]
    copies = [pltpu.make_async_copy(a, b, sem.at[i]) for i, (a, b) in enumerate(loads)]
    for copy in copies:
        copy.start()

    l_before, l_after = boundary(lengths_ref, first)
    r_before, r_after = boundary(lengths_ref, last)
    l_shared = jnp.logical_and(l_before == 2, l_after == 2)
    r_shared = jnp.logical_and(r_before == 2, r_after == 2)
    l_away = l_after == 1
    l_here = jnp.logical_and(l_before == 1, l_after > 1)
    r_here = r_after == 1
    r_away = jnp.logical_and(r_before == 1, r_after > 1)
    for i, flag in enumerate((l_away, l_shared, r_away, r_shared)):
        flags_out[i] = flag.astype(jnp.int32)

    def collect(i, carry):
        start, number = carry
        end = start + lengths_ref[0, i]
        on_left = jnp.logical_and(start < first, end > first)
        on_right = jnp.logical_and(start < last, end > last)
        within = jnp.logical_and(start >= first, end <= last)
        mine = jnp.logical_or(
            within,
            jnp.logical_or(
                jnp.logical_and(on_left, jnp.logical_not(l_away)),
                jnp.logical_and(on_right, jnp.logical_not(r_away)),
            ),
        )
        shared = jnp.logical_or(
            jnp.logical_and(on_left, l_shared), jnp.logical_and(on_right, r_shared)
        )

        @pl.when(mine)
        def _():
            work[number, 0] = jnp.where(shared, 5, end - start)
            work[number, 1] = start - first + 2

        return end, number + mine.astype(jnp.int32)

    _, number = lax.fori_loop(
        0, lengths_ref.shape[1], collect, (jnp.int32(0), jnp.int32(0))
    )
    for copy in copies:
        copy.wait()

    for side, (here, slot) in enumerate(((l_here, 1), (r_here, 6))):
        @pl.when(here)
        def _():
            dm_buf[block(slot)] = dot(dy_buf[side], w_buf[...], NT).astype(jnp.bfloat16)

    bufs = (q_buf, k_buf, v_buf, dm_buf, mixed, gq, gk, gv)

    def image(i, carry):
        kind, at = work[i, 0], work[i, 1]
        for blocks in range(1, OWN + 1):
            @pl.when(kind == blocks)
            def _():
                attend(*bufs, at, blocks, at, blocks)

        @pl.when(kind == 5)
        def _():
            attend(*bufs, jnp.where(at == 0, 2, 4), 2, at, 4)

        return carry

    lax.fori_loop(0, number, image, 0)

    idle = (
        (jnp.logical_not(l_here), 1), (l_away, 2), (r_away, 5), (jnp.logical_not(r_here), 6)
    )
    for flag, slot in idle:
        @pl.when(flag)
        def _():
            mixed[block(slot)] = jnp.zeros((BLOCK, D), jnp.bfloat16)

    stores = [
        (mixed.at[pl.ds(BLOCK, 6 * BLOCK)], mixed_out),
        (gq.at[own], gq_out), (gk.at[own], gk_out), (gv.at[own], gv_out),
    ]
    for side, near in enumerate((1, 6)):
        stores += [
            (gk.at[block(near)], ret_out.at[side, 0]), (gv.at[block(near)], ret_out.at[side, 1]),
        ]
    outs = [pltpu.make_async_copy(a, b, sem.at[i]) for i, (a, b) in enumerate(stores)]
    for copy in outs:
        copy.start()
    for side, (here, slot) in enumerate(((l_here, 1), (r_here, 6))):
        @pl.when(here)
        def _():
            att[side] = dot(mixed[block(slot)], w_buf[...], NN).astype(jnp.bfloat16)

    for side, (near, far, shared) in enumerate(((1, 0, l_shared), (6, 7, r_shared))):
        choices = (
            (gk.at[block(far)], gq.at[block(near)]), (gv.at[block(far)], att.at[side])
        )
        for at, (if_shared, if_moved) in enumerate(choices):
            index = len(stores) + 2 * side + at
            to = ret_out.at[side, 2 + at]

            @pl.when(shared)
            def _():
                pltpu.make_async_copy(if_shared, to, sem.at[index]).start()

            @pl.when(jnp.logical_not(shared))
            def _():
                pltpu.make_async_copy(if_moved, to, sem.at[index]).start()

    for side in range(2):
        for at in range(2):
            index = len(stores) + 2 * side + at
            pltpu.make_async_copy(
                gk.at[block(0)], ret_out.at[side, 2 + at], sem.at[index]
            ).wait()
    for copy in outs:
        copy.wait()


def finish_kernel(
    count, ret_ref, mixed_ref, dy_ref, halo_ref, w_ref, back_ref, sum_ref, att_ref,
    mixed, dy, w_buf, acc, stage, parts, sibling, total, second, half, third, whole, fourth, fifth,
    load_sem, ret_send, ret_recv, one_send, one_recv, sends, recvs,
):
    left, right = ring_neighbours(count)
    me, y = lax.axis_index("tok"), lax.axis_index("dp")
    core, z, x = lax.rem(me, 2), lax.rem(me // 2, SIDE), me // (2 * SIDE)
    loads = [
        (mixed_ref, mixed),
        (halo_ref.at[0, 3], dy.at[pl.ds(0, BLOCK)]),
        (dy_ref, dy.at[pl.ds(BLOCK, OWN * BLOCK)]),
        (halo_ref.at[1, 3], dy.at[pl.ds((OWN + 1) * BLOCK, BLOCK)]),
        (w_ref, w_buf),
    ]
    loads = [pltpu.make_async_copy(a, b, load_sem.at[i]) for i, (a, b) in enumerate(loads)]
    for load in loads:
        load.start()

    def device(x, y, z, core):
        return {"dp": y, "tok": (x * SIDE + z) * 2 + core}

    def turned(at, step):
        return lax.rem(at + step, SIDE)

    other = device(x, y, z, 1 - core)
    steps = range(1, SIDE)
    along_x = [device(turned(x, step), y, z, core) for step in steps]
    along_y = [device(x, turned(y, step), z, core) for step in steps]
    along_z = [device(x, y, turned(z, step), core) for step in steps]
    greet([left, right, other] + along_x + along_y + along_z)

    def remote(source, landing, send_sem, recv_sem, where):
        return pltpu.make_async_remote_copy(
            src_ref=source, dst_ref=landing, send_sem=send_sem, recv_sem=recv_sem,
            device_id=where, device_id_type=MESH,
        )

    copies = []
    for side in range(2):
        for slot in range(4):
            copy = remote(
                ret_ref.at[side, slot], back_ref.at[1 - side, slot],
                ret_send.at[side, slot], ret_recv.at[1 - side, slot],
                {"tok": right if side else left},
            )
            copy.start()
            copies.append(copy)

    for load in loads[:-1]:
        load.wait()
    stage[...] = jnp.zeros_like(stage)
    one = []
    for piece in range(PIECES):
        columns = slice(piece * PIECE, (piece + 1) * PIECE)

        def weight(i, carry):
            lanes = pl.ds(pl.multiple_of(i * 128, 128), 128)
            acc[lanes] = dot(mixed[:, lanes], dy[:, columns], TN)
            return carry

        lax.fori_loop(0, D // 128, weight, 0)
        for part in range(D // PART):
            px, pz, pcore = part // 8, part // 2 % 4, part % 2
            place = (pz, px) if pcore else (px, pz)
            for tile in range(PIECE // 128):
                stage[tile * PART : (tile + 1) * PART] = acc[
                    part * PART : (part + 1) * PART, tile * 128 : (tile + 1) * 128
                ]
            parts[piece, pcore, place[0], place[1]] = stage[...].astype(jnp.bfloat16)
        copy = remote(
            parts.at[piece, 1 - core], sibling.at[piece], one_send.at[piece], one_recv.at[piece],
            other,
        )
        copy.start()
        one.append(copy)

    def spread(stage_at, piece, source, landing, x_axis):
        at = jnp.where(x_axis, x, y)
        started = []
        for step in steps:
            there = turned(at, step)
            where = device(jnp.where(x_axis, there, x), jnp.where(x_axis, y, there), z, core)
            copy = remote(
                source.at[there], landing.at[step - 1],
                sends.at[stage_at, piece, step - 1], recvs.at[stage_at, piece, step - 1], where,
            )
            copy.start()
            started.append(copy)
        return at, started

    def add(*values):
        result = values[0].astype(jnp.float32)
        for value in values[1:]:
            result = result + value.astype(jnp.float32)
        return result.astype(jnp.bfloat16)

    twos = []
    for piece in range(PIECES):
        one[piece].wait()
        for row in range(SIDE):
            total[piece, row] = add(parts[piece, core, row], sibling[piece, row])
        twos.append(spread(0, piece, total.at[piece], second.at[piece], core == 0))

    loads[-1].wait()
    for part in range(OWN):
        rows = slice(part * BLOCK, (part + 1) * BLOCK)
        ours = mixed[(part + 1) * BLOCK : (part + 2) * BLOCK]
        att_ref[rows] = dot(ours, w_buf[...], NN).astype(jnp.bfloat16)

    threes = []
    for piece in range(PIECES):
        at, started = twos[piece]
        for copy in started:
            copy.wait()
        half[piece] = add(total[piece, at], *[second[piece, step - 1] for step in steps])
        threes.append(spread(1, piece, half.at[piece], third.at[piece], core == 1))

    gap = lax.rem(z - y + SIDE, SIDE)

    def to_plane(piece, step):
        return remote(
            whole.at[piece], fourth.at[piece, step - 1],
            sends.at[2, piece, step - 1], recvs.at[2, piece, step - 1],
            device(x, y, turned(z, SIDE - step), core),
        )

    def to_row(piece, step):
        return remote(
            fifth.at[0, piece], fifth.at[1, piece],
            sends.at[3, piece, step - 1], recvs.at[3, piece, 0],
            device(x, turned(y, step), z, core),
        )

    for piece in range(PIECES):
        at, started = threes[piece]
        for copy in started:
            copy.wait()
        whole[piece] = add(half[piece, at], *[third[piece, step - 1] for step in steps])
        for step in steps:
            @pl.when(gap == step)
            def _():
                to_plane(piece, step).start()

    @pl.when(gap == 0)
    def _():
        for piece in range(PIECES):
            for step in steps:
                to_plane(piece, step).wait_recv()
            fifth[0, piece] = add(whole[piece], *[fourth[piece, step - 1] for step in steps])
            for step in steps:
                to_row(piece, step).start()
        for piece in range(PIECES):
            for step in steps:
                to_row(piece, step).wait_send()
        sum_ref[...] = fifth[0]

    @pl.when(gap != 0)
    def _():
        for piece in range(PIECES):
            to_row(piece, 1).wait_recv()
        sum_ref[...] = fifth[1]

    for piece in range(PIECES):
        for step in steps:
            @pl.when(gap == step)
            def _():
                to_plane(piece, step).wait_send()

    for copy in copies:
        copy.wait()


def settle_kernel(
    norm, flags_ref, sum_ref, back_ref, att_in, gq_in, gk_in, gv_in,
    att_out, gq_out, gk_out, gv_out, rows_ref, own, extra, sem,
):
    def block(i):
        return pl.ds(i * BLOCK, BLOCK)

    sides = []
    for side, (near, far) in enumerate(((0, 1), (3, 2))):
        parts = ((gk_out, near, 0), (gv_out, near, 1), (gk_out, far, 2), (gv_out, far, 3))
        ours = [
            pltpu.make_async_copy(out.at[block(at)], own.at[side, slot], sem.at[side, slot])
            for out, at, slot in parts
        ]
        theirs = [
            pltpu.make_async_copy(
                back_ref.at[side, slot], extra.at[side, slot], sem.at[side, 4 + slot]
            )
            for slot in range(4)
        ]
        moved = [
            pltpu.make_async_copy(extra.at[side, slot], out.at[block(near)], sem.at[side, slot])
            for slot, out in enumerate((gk_out, gv_out, gq_out, att_out))
        ]
        added = [
            pltpu.make_async_copy(own.at[side, slot], out.at[block(at)], sem.at[side, slot])
            for out, at, slot in parts
        ]
        away, shared = flags_ref[2 * side] == 1, flags_ref[2 * side + 1] == 1
        sides.append((side, ours, theirs, moved, added, away, shared))

    for side, ours, theirs, moved, added, away, shared in sides:
        for copy in theirs:
            copy.start()

        @pl.when(shared)
        def _():
            for copy in ours:
                copy.start()

    for piece in range(PIECES):
        for tile in range(PIECE // 128):
            lanes = slice(piece * PIECE + tile * 128, piece * PIECE + (tile + 1) * 128)
            part = sum_ref[piece].astype(jnp.float32)[tile * PART : (tile + 1) * PART]
            rows_ref[:, lanes] = part * norm

    for side, ours, theirs, moved, added, away, shared in sides:
        for copy in theirs:
            copy.wait()

        @pl.when(away)
        def _():
            for copy in moved:
                copy.start()

        @pl.when(shared)
        def _():
            for slot in range(4):
                ours[slot].wait()
                both = own[side, slot].astype(jnp.float32) + extra[side, slot].astype(jnp.float32)
                own[side, slot] = both.astype(jnp.bfloat16)
                added[slot].start()

    for side, ours, theirs, moved, added, away, shared in sides:
        @pl.when(jnp.logical_or(away, shared))
        def _():
            for copy in added:
                copy.wait()


def on_device(q_tokens, k_tokens, v_tokens, d_attended, w_out, lengths):
    rows, width = q_tokens.shape[1:]
    count = lax.axis_size("tok")
    norm = 1.0 / math.sqrt(lax.axis_size("dp") * count * rows)
    q, k, v, dy = q_tokens[0], k_tokens[0], v_tokens[0], d_attended[0]
    low = jnp.bfloat16
    vmem, smem, anywhere = (
        pl.BlockSpec(memory_space=space) for space in (pltpu.VMEM, pltpu.SMEM, pl.ANY)
    )
    token_shape = jax.ShapeDtypeStruct((rows, width), low)
    halo_shape = jax.ShapeDtypeStruct((2, 4, BLOCK, width), low)
    big = 58 * 1024 * 1024

    halo, dm = pl.pallas_call(
        functools.partial(exchange_kernel, count),
        out_shape=(halo_shape, token_shape),
        in_specs=[smem] + [anywhere] * 5,
        out_specs=(anywhere, vmem),
        scratch_shapes=[
            pltpu.VMEM((rows, width), low),
            pltpu.VMEM((width, width), low),
            pltpu.VMEM((2, BLOCK, width), low),
            pltpu.VMEM((2, 2, BLOCK, width), low),
            pltpu.VMEM((2, 2, BLOCK, width), low),
            pltpu.SemaphoreType.DMA((8,)),
            pltpu.SemaphoreType.DMA((2, 4)),
            pltpu.SemaphoreType.DMA((2, 4)),
        ],
        compiler_params=pltpu.CompilerParams(
            collective_id=0, has_side_effects=True, vmem_limit_bytes=big
        ),
        name="exchange",
    )(lengths, q, k, v, dy, w_out)

    dma = pltpu.SemaphoreType.DMA
    slab = pltpu.VMEM((SLOTS * BLOCK, width), low)
    square = pltpu.VMEM((width, width), low)
    sides = pltpu.VMEM((2, BLOCK, width), low)
    mixed_shape = jax.ShapeDtypeStruct(((OWN + 2) * BLOCK, width), low)
    mixed, gq, gk, gv, ret, flags = pl.pallas_call(
        attention_kernel,
        out_shape=(
            mixed_shape, token_shape, token_shape, token_shape, halo_shape,
            jax.ShapeDtypeStruct((4,), jnp.int32),
        ),
        in_specs=[smem] + [anywhere] * 6,
        out_specs=(anywhere,) * 5 + (smem,),
        scratch_shapes=[slab] * 4 + [square, sides] + [slab] * 4
        + [sides, pltpu.SMEM((8, 2), jnp.int32), dma((17,))],
        compiler_params=pltpu.CompilerParams(vmem_limit_bytes=big),
        name="attention",
    )(lengths, q, k, v, dm, halo, w_out)

    sum_shape = jax.ShapeDtypeStruct((PIECES, PACKED, 128), low)

    def pieces(*sizes):
        return pltpu.VMEM((PIECES, *sizes, PACKED, 128), low)

    slab = pltpu.VMEM(mixed_shape.shape, low)
    back, summed, att = pl.pallas_call(
        functools.partial(finish_kernel, count),
        out_shape=(halo_shape, sum_shape, token_shape),
        in_specs=[anywhere] * 5,
        out_specs=(anywhere, vmem, vmem),
        scratch_shapes=[
            slab, slab, square,
            pltpu.VMEM((width, PIECE), jnp.float32),
            pltpu.VMEM((PACKED, 128), jnp.float32),
            pieces(2, SIDE, SIDE), pieces(SIDE, SIDE), pieces(SIDE, SIDE),
            pieces(SIDE - 1, SIDE), pieces(SIDE), pieces(SIDE - 1),
            pieces(), pieces(SIDE - 1),
            pltpu.VMEM((2, PIECES, PACKED, 128), low),
            dma((5,)), dma((2, 4)), dma((2, 4)), dma((PIECES,)), dma((PIECES,)),
            dma((4, PIECES, SIDE - 1)), dma((4, PIECES, SIDE - 1)),
        ],
        compiler_params=pltpu.CompilerParams(
            collective_id=1, has_side_effects=True, vmem_limit_bytes=big
        ),
        name="finish",
    )(ret, mixed, dy, halo, w_out)

    att, gq, gk, gv, grad_rows = pl.pallas_call(
        functools.partial(settle_kernel, norm),
        out_shape=(token_shape,) * 4 + (jax.ShapeDtypeStruct((PART, width), jnp.float32),),
        in_specs=[smem, vmem] + [anywhere] * 5,
        out_specs=(anywhere,) * 4 + (vmem,),
        scratch_shapes=[
            pltpu.VMEM((2, 4, BLOCK, width), low),
            pltpu.VMEM((2, 4, BLOCK, width), low),
            dma((2, 8)),
        ],
        input_output_aliases={3: 0, 4: 1, 5: 2, 6: 3},
        compiler_params=pltpu.CompilerParams(vmem_limit_bytes=big),
        name="settle",
    )(flags, summed, back, att, gq, gk, gv)
    return (att[None], gq[None], gk[None], gv[None], grad_rows)


def solution(mesh):
    tokens = P("dp", "tok", None)
    return jax.shard_map(
        on_device,
        mesh=mesh,
        in_specs=(tokens, tokens, tokens, tokens, P(), P("dp", None)),
        out_specs=(tokens, tokens, tokens, tokens, P("tok", None)),
        check_vma=False,
    )
```

time: 121 us -> 105 us (0.87); the launches traced: 121 us -> 104 us
  Pallas kernels: 120 us -> 101 us
  local copies, waits for them, and re-layouts: 0 us -> 2.37 us
    pallas_call x1, Pallas kernels: 67.8 us -> 55.1 us  [on_device(): pl.pallas_call(functools.partial(finish_kernel, count), out_shape=(halo_s...]
    pallas_call x1, Pallas kernels: 30.3 us -> 24.2 us  [on_device(): pl.pallas_call(attention_kernel, out_shape=(mixed_shape, token_shape, tok...]
    unnamed x0 -> x1, local copies, waits for them, and re-layouts: none -> 2.37 us
where the time goes in v3:
time: 105 us; the launch traced here: 104 us
  Pallas kernels  101 us (96%)
  local copies, waits for them, and re-layouts  2.37 us (2%)
    pallas_call x1, Pallas kernels, on_device(): pl.pallas_call(functools.partial(finish_kernel, count), out_shape=(halo_s...  55.1 us
    pallas_call x1, Pallas kernels, on_device(): pl.pallas_call(attention_kernel, out_shape=(mixed_shape, token_shape, tok...  24.2 us
    pallas_call x1, Pallas kernels, on_device(): pl.pallas_call(functools.partial(exchange_kernel, count), out_shape=(halo...  18 us
    pallas_call x1, Pallas kernels, on_device(): pl.pallas_call(functools.partial(settle_kernel, norm), out_shape=(token_s...  3.3 us
    unnamed x1, local copies, waits for them, and re-layouts  2.37 us

profile of v3, /device:TPU:64, one launch (start us, length us, event | category | flops | bytes accessed | tf_op | source)
XLA Modules:
  0.0 103.6 jit_solution(18202080329478860082)
XLA Ops:
  0.6 18.0 %exchange.1 = (bf16[2,4,128,1152]{3,2,1,0:T(8,128)(2,1)}, bf16[512,1152]{1,0:T(8,128)(2,1)}) custom-call(s32[1,64]{1,0:T(1,128)} %lengths_ref.3, bf16[512,1152]{1,0:T(8,128)(2,1)} %bitcast.9, bf16[512,1152]{1,0:T(8,128)(2,1)} %bitcast.11, bf16[512,1152]{1,0:T(8,128)(2,1)} %bitcast.13, bf16[512,1152]{1,0:T(8,128)(2,1)} %bitcast.15, bf16[1152,1152]{1,0:T(8,128)(2,1)} %w_ref.5), custom_call_target="tpu_custom_call" | custom-call | tf_op jit(solution)/shard_map/exchange/pallas_call | solution.py:555
  18.6 24.2 %attention.1 = (bf16[768,1152]{1,0:T(8,128)(2,1)}, bf16[512,1152]{1,0:T(8,128)(2,1)}, bf16[512,1152]{1,0:T(8,128)(2,1)}, bf16[512,1152]{1,0:T(8,128)(2,1)}, bf16[2,4,128,1152]{3,2,1,0:T(8,128)(2,1)}, /*index=5*/s32[4]{0:T(128)}) custom-call(s32[1,64]{1,0:T(1,128)} %lengths_ref.3, bf16[512,1152]{1,0:T(8,128)(2,1)} %bitcast.10, bf16[512,1152]{1,0:T(8,128)(2,1)} %bitcast.12, ...), custom_call_target="tpu_custom_call" | custom-call | tf_op jit(solution)/shard_map/attention/pallas_call | solution.py:581
  42.8 55.1 %finish.1 = (bf16[2,4,128,1152]{3,2,1,0:T(8,128)(2,1)}, bf16[3,112,128]{2,1,0:T(8,128)(2,1)}, bf16[512,1152]{1,0:T(8,128)(2,1)}) custom-call(bf16[2,4,128,1152]{3,2,1,0:T(8,128)(2,1)} %get-tuple-element.24.ret_ref, bf16[768,1152]{1,0:T(8,128)(2,1)} %get-tuple-element.25.mixed_ref, bf16[512,1152]{1,0:T(8,128)(2,1)} %bitcast.16, ...), custom_call_target="tpu_custom_call" | custom-call | tf_op jit(solution)/shard_map/finish/pallas_call | solution.py:601
  97.9 3.3 %settle.1 = (bf16[512,1152]{1,0:T(8,128)(2,1)}, bf16[512,1152]{1,0:T(8,128)(2,1)}, bf16[512,1152]{1,0:T(8,128)(2,1)}, bf16[512,1152]{1,0:T(8,128)(2,1)}, f32[36,1152]{1,0:T(8,128)}) custom-call(s32[4]{0:T(128)} %get-tuple-element.23.flags_ref, ...), custom_call_target="tpu_custom_call", output_to_operand_aliasing={{0}: (3, {}), {1}: (4, {}), {2}: (5, {}), {3}: (6, {})} | custom-call | tf_op jit(solution)/shard_map/settle/pallas_call | solution.py:623
  101.2 2.4 %copy.20 = bf16[1,512,1152]{2,1,0:T(8,128)(2,1)} copy(bf16[1,512,1152]{2,1,0:T(8,128)(2,1)} %bitcast.8) | data formatting | bytes 2359296

commit v4 on v3

--- a/solution.py
+++ b/solution.py
@@ -45,11 +45,15 @@
 
 
 def greet(others):
-    barrier = pltpu.get_barrier_semaphore()
     for other in others:
         where = other if isinstance(other, dict) else {"tok": other}
-        pl.semaphore_signal(barrier, inc=1, device_id=where, device_id_type=MESH)
-    pl.semaphore_wait(barrier, len(others))
+        pl.semaphore_signal(
+            pltpu.get_barrier_semaphore(), inc=1, device_id=where, device_id_type=MESH
+        )
+
+
+def meet(others):
+    pl.semaphore_wait(pltpu.get_barrier_semaphore(), len(others))
 
 
 def ring_neighbours(count):
@@ -77,6 +81,7 @@
     for load in loads:
         load.start()
     greet((left, right))
+    meet((left, right))
     copies = []
 
     def send(side, slot, source):
@@ -157,7 +162,7 @@
 def attention_kernel(
     lengths_ref, q_ref, k_ref, v_ref, dm_ref, halo_ref, w_ref,
     mixed_out, gq_out, gk_out, gv_out, ret_out, flags_out,
-    q_buf, k_buf, v_buf, dm_buf, w_buf, dy_buf, mixed, gq, gk, gv, att, work, sem,
+    q_buf, k_buf, v_buf, dm_buf, w_buf, dy_buf, mixed, gq, gk, gv, att, work, sem, halo_sem, store_sem,
 ):
     first = lax.axis_index("tok") * OWN
     last = first + OWN
@@ -170,18 +175,10 @@
         (q_ref, q_buf.at[own]), (k_ref, k_buf.at[own]), (v_ref, v_buf.at[own]),
         (dm_ref, dm_buf.at[own]), (w_ref, w_buf),
     ]
-    for side, (near, far) in enumerate(((1, 0), (6, 7))):
-        loads += [
-            (halo_ref.at[side, 0], k_buf.at[block(near)]),
-            (halo_ref.at[side, 1], v_buf.at[block(near)]),
-            (halo_ref.at[side, 2], q_buf.at[block(near)]),
-            (halo_ref.at[side, 2], k_buf.at[block(far)]),
-            (halo_ref.at[side, 3], dy_buf.at[side]),
-            (halo_ref.at[side, 3], v_buf.at[block(far)]),
-        ]
-    copies = [pltpu.make_async_copy(a, b, sem.at[i]) for i, (a, b) in enumerate(loads)]
-    for copy in copies:
-        copy.start()
+    loads = [pltpu.make_async_copy(a, b, sem.at[i]) for i, (a, b) in enumerate(loads)]
+    w_load = loads.pop()
+    for load in loads:
+        load.start()
 
     l_before, l_after = boundary(lengths_ref, first)
     r_before, r_after = boundary(lengths_ref, last)
@@ -193,6 +190,25 @@
     r_away = jnp.logical_and(r_before == 1, r_after > 1)
     for i, flag in enumerate((l_away, l_shared, r_away, r_shared)):
         flags_out[i] = flag.astype(jnp.int32)
+
+    halo_loads = []
+    for side, (near, far, here, shared) in enumerate(
+        ((1, 0, l_here, l_shared), (6, 7, r_here, r_shared))
+    ):
+        def load(slot, to, side=side):
+            return pltpu.make_async_copy(halo_ref.at[side, slot], to, halo_sem.at[side, slot])
+
+        both = [load(0, k_buf.at[block(near)]), load(1, v_buf.at[block(near)])]
+        if_here = [load(2, q_buf.at[block(near)]), load(3, dy_buf.at[side])]
+        if_shared = [load(2, k_buf.at[block(far)]), load(3, v_buf.at[block(far)])]
+        halo_loads += [(here, both + if_here), (shared, both + if_shared)]
+    for flag, some in halo_loads:
+        @pl.when(flag)
+        def _():
+            for load in some:
+                load.start()
+
+    w_load.start()
 
     def collect(i, carry):
         start, number = carry
@@ -221,15 +237,43 @@
     _, number = lax.fori_loop(
         0, lengths_ref.shape[1], collect, (jnp.int32(0), jnp.int32(0))
     )
-    for copy in copies:
-        copy.wait()
-
+    for load in loads:
+        load.wait()
+    for flag, some in halo_loads:
+        @pl.when(flag)
+        def _():
+            for load in some:
+                load.wait()
+
+    w_load.wait()
     for side, (here, slot) in enumerate(((l_here, 1), (r_here, 6))):
         @pl.when(here)
         def _():
             dm_buf[block(slot)] = dot(dy_buf[side], w_buf[...], NT).astype(jnp.bfloat16)
 
     bufs = (q_buf, k_buf, v_buf, dm_buf, mixed, gq, gk, gv)
+
+    def store(index, slot):
+        if index == 0:
+            return pltpu.make_async_copy(
+                mixed.at[rows_of(slot)], mixed_out.at[rows_of(slot - 1)], store_sem.at[0, slot]
+            )
+        ref, out = ((gq, gq_out), (gk, gk_out), (gv, gv_out))[index - 1]
+        return pltpu.make_async_copy(
+            ref.at[rows_of(slot)], out.at[rows_of(slot - 2)], store_sem.at[index, slot]
+        )
+
+    def rows_of(slot):
+        return pl.ds(pl.multiple_of(slot * BLOCK, BLOCK), BLOCK)
+
+    def store_all(slot, indices):
+        for index in indices:
+            if index == 0:
+                store(0, slot).start()
+            else:
+                @pl.when(jnp.logical_and(slot >= 2, slot < 2 + OWN))
+                def _():
+                    store(index, slot).start()
 
     def image(i, carry):
         kind, at = work[i, 0], work[i, 1]
@@ -237,10 +281,15 @@
             @pl.when(kind == blocks)
             def _():
                 attend(*bufs, at, blocks, at, blocks)
+                for j in range(blocks):
+                    store_all(at + j, range(4))
 
         @pl.when(kind == 5)
         def _():
-            attend(*bufs, jnp.where(at == 0, 2, 4), 2, at, 4)
+            q_at = jnp.where(at == 0, 2, 4)
+            attend(*bufs, q_at, 2, at, 4)
+            for j in range(2):
+                store_all(q_at + j, range(4))
 
         return carry
 
@@ -253,52 +302,47 @@
         @pl.when(flag)
         def _():
             mixed[block(slot)] = jnp.zeros((BLOCK, D), jnp.bfloat16)
-
-    stores = [
-        (mixed.at[pl.ds(BLOCK, 6 * BLOCK)], mixed_out),
-        (gq.at[own], gq_out), (gk.at[own], gk_out), (gv.at[own], gv_out),
-    ]
-    for side, near in enumerate((1, 6)):
-        stores += [
-            (gk.at[block(near)], ret_out.at[side, 0]), (gv.at[block(near)], ret_out.at[side, 1]),
-        ]
-    outs = [pltpu.make_async_copy(a, b, sem.at[i]) for i, (a, b) in enumerate(stores)]
-    for copy in outs:
-        copy.start()
-    for side, (here, slot) in enumerate(((l_here, 1), (r_here, 6))):
+            store_all(jnp.int32(slot), range(4))
+
+    def give(side, slot, source):
+        return pltpu.make_async_copy(source, ret_out.at[side, slot], halo_sem.at[side, slot])
+
+    gives = []
+    for side, (near, far, here, shared) in enumerate(
+        ((1, 0, l_here, l_shared), (6, 7, r_here, r_shared))
+    ):
+        both = [give(side, 0, gk.at[block(near)]), give(side, 1, gv.at[block(near)])]
+        if_here = [give(side, 2, gq.at[block(near)]), give(side, 3, att.at[side])]
+        if_shared = [give(side, 2, gk.at[block(far)]), give(side, 3, gv.at[block(far)])]
+
         @pl.when(here)
         def _():
-            att[side] = dot(mixed[block(slot)], w_buf[...], NN).astype(jnp.bfloat16)
-
-    for side, (near, far, shared) in enumerate(((1, 0, l_shared), (6, 7, r_shared))):
-        choices = (
-            (gk.at[block(far)], gq.at[block(near)]), (gv.at[block(far)], att.at[side])
-        )
-        for at, (if_shared, if_moved) in enumerate(choices):
-            index = len(stores) + 2 * side + at
-            to = ret_out.at[side, 2 + at]
-
-            @pl.when(shared)
-            def _():
-                pltpu.make_async_copy(if_shared, to, sem.at[index]).start()
-
-            @pl.when(jnp.logical_not(shared))
-            def _():
-                pltpu.make_async_copy(if_moved, to, sem.at[index]).start()
-
-    for side in range(2):
-        for at in range(2):
-            index = len(stores) + 2 * side + at
-            pltpu.make_async_copy(
-                gk.at[block(0)], ret_out.at[side, 2 + at], sem.at[index]
-            ).wait()
-    for copy in outs:
-        copy.wait()
+            for copy in both + if_here[:1]:
+                copy.start()
+            att[side] = dot(mixed[block(near)], w_buf[...], NN).astype(jnp.bfloat16)
+            if_here[1].start()
+
+        @pl.when(shared)
+        def _():
+            for copy in both + if_shared:
+                copy.start()
+
+        gives += [(here, both + if_here), (shared, both + if_shared)]
+    for flag, some in gives:
+        @pl.when(flag)
+        def _():
+            for copy in some:
+                copy.wait()
+
+    for slot in range(1, 3 + OWN):
+        for index in range(4):
+            if index == 0 or 2 <= slot < 2 + OWN:
+                store(index, slot).wait()
 
 
 def finish_kernel(
     count, ret_ref, mixed_ref, dy_ref, halo_ref, w_ref, back_ref, sum_ref, att_ref,
-    mixed, dy, w_buf, acc, stage, parts, sibling, total, second, half, third, whole, fourth, fifth,
+    mixed, turned_mixed, dy, w_buf, att, acc, stage, parts, sibling, total, second, half, third, whole, fourth, fifth,
     load_sem, ret_send, ret_recv, one_send, one_recv, sends, recvs,
 ):
     left, right = ring_neighbours(count)
@@ -326,7 +370,9 @@
     along_x = [device(turned(x, step), y, z, core) for step in steps]
     along_y = [device(x, turned(y, step), z, core) for step in steps]
     along_z = [device(x, y, turned(z, step), core) for step in steps]
-    greet([left, right, other] + along_x + along_y + along_z)
+    others = [left, right, other] + along_x + along_y + along_z
+    greet(others)
+    copies = []
 
     def remote(source, landing, send_sem, recv_sem, where):
         return pltpu.make_async_remote_copy(
@@ -334,30 +380,28 @@
             device_id=where, device_id_type=MESH,
         )
 
-    copies = []
-    for side in range(2):
-        for slot in range(4):
-            copy = remote(
-                ret_ref.at[side, slot], back_ref.at[1 - side, slot],
-                ret_send.at[side, slot], ret_recv.at[1 - side, slot],
-                {"tok": right if side else left},
-            )
-            copy.start()
-            copies.append(copy)
+    def send(*args):
+        copy = remote(*args)
+        copy.start()
+        copies.append(copy)
+        return copy
 
     for load in loads[:-1]:
         load.wait()
+    for tile in range(D // 128):
+        lanes = slice(tile * 128, (tile + 1) * 128)
+        turned_mixed[lanes] = mixed[:, lanes].T
     stage[...] = jnp.zeros_like(stage)
-    one = []
-    for piece in range(PIECES):
+
+    def product(piece):
         columns = slice(piece * PIECE, (piece + 1) * PIECE)
 
         def weight(i, carry):
-            lanes = pl.ds(pl.multiple_of(i * 128, 128), 128)
-            acc[lanes] = dot(mixed[:, lanes], dy[:, columns], TN)
+            at = pl.ds(pl.multiple_of(i * PIECE, PIECE), PIECE)
+            acc[at] = dot(turned_mixed[at], dy[:, columns], NN)
             return carry
 
-        lax.fori_loop(0, D // 128, weight, 0)
+        lax.fori_loop(0, D // PIECE, weight, 0)
         for part in range(D // PART):
             px, pz, pcore = part // 8, part // 2 % 4, part % 2
             place = (pz, px) if pcore else (px, pz)
@@ -366,12 +410,12 @@
                     part * PART : (part + 1) * PART, tile * 128 : (tile + 1) * 128
                 ]
             parts[piece, pcore, place[0], place[1]] = stage[...].astype(jnp.bfloat16)
-        copy = remote(
+
+    def to_sibling(piece):
+        return send(
             parts.at[piece, 1 - core], sibling.at[piece], one_send.at[piece], one_recv.at[piece],
             other,
         )
-        copy.start()
-        one.append(copy)
 
     def spread(stage_at, piece, source, landing, x_axis):
         at = jnp.where(x_axis, x, y)
@@ -379,12 +423,10 @@
         for step in steps:
             there = turned(at, step)
             where = device(jnp.where(x_axis, there, x), jnp.where(x_axis, y, there), z, core)
-            copy = remote(
+            started.append(send(
                 source.at[there], landing.at[step - 1],
                 sends.at[stage_at, piece, step - 1], recvs.at[stage_at, piece, step - 1], where,
-            )
-            copy.start()
-            started.append(copy)
+            ))
         return at, started
 
     def add(*values):
@@ -393,26 +435,47 @@
             result = result + value.astype(jnp.float32)
         return result.astype(jnp.bfloat16)
 
-    twos = []
-    for piece in range(PIECES):
-        one[piece].wait()
+    twos, threes = [], []
+
+    def second_stage(piece):
+        one[piece].wait_recv()
         for row in range(SIDE):
             total[piece, row] = add(parts[piece, core, row], sibling[piece, row])
         twos.append(spread(0, piece, total.at[piece], second.at[piece], core == 0))
+
+    def third_stage(piece):
+        at, started = twos[piece]
+        for copy in started:
+            copy.wait_recv()
+        half[piece] = add(total[piece, at], *[second[piece, step - 1] for step in steps])
+        threes.append(spread(1, piece, half.at[piece], third.at[piece], core == 1))
+
+    product(0)
+    meet(others)
+    one = [to_sibling(0)]
+    returns = []
+    for side in range(2):
+        for slot in range(4):
+            returns.append(send(
+                ret_ref.at[side, slot], back_ref.at[1 - side, slot],
+                ret_send.at[side, slot], ret_recv.at[1 - side, slot],
+                {"tok": right if side else left},
+            ))
+    for piece in range(1, PIECES):
+        product(piece)
+        one.append(to_sibling(piece))
+        second_stage(piece - 1)
+    second_stage(PIECES - 1)
 
     loads[-1].wait()
     for part in range(OWN):
         rows = slice(part * BLOCK, (part + 1) * BLOCK)
         ours = mixed[(part + 1) * BLOCK : (part + 2) * BLOCK]
-        att_ref[rows] = dot(ours, w_buf[...], NN).astype(jnp.bfloat16)
-
-    threes = []
+        att[rows] = dot(ours, w_buf[...], NN).astype(jnp.bfloat16)
+    att_store = pltpu.make_async_copy(att, att_ref, load_sem.at[0])
+    att_store.start()
     for piece in range(PIECES):
-        at, started = twos[piece]
-        for copy in started:
-            copy.wait()
-        half[piece] = add(total[piece, at], *[second[piece, step - 1] for step in steps])
-        threes.append(spread(1, piece, half.at[piece], third.at[piece], core == 1))
+        third_stage(piece)
 
     gap = lax.rem(z - y + SIDE, SIDE)
 
@@ -433,7 +496,7 @@
     for piece in range(PIECES):
         at, started = threes[piece]
         for copy in started:
-            copy.wait()
+            copy.wait_recv()
         whole[piece] = add(half[piece, at], *[third[piece, step - 1] for step in steps])
         for step in steps:
             @pl.when(gap == step)
@@ -465,17 +528,22 @@
             def _():
                 to_plane(piece, step).wait_send()
 
+    for copy in returns:
+        copy.wait_recv()
     for copy in copies:
-        copy.wait()
+        copy.wait_send()
+    att_store.wait()
 
 
 def settle_kernel(
     norm, flags_ref, sum_ref, back_ref, att_in, gq_in, gk_in, gv_in,
-    att_out, gq_out, gk_out, gv_out, rows_ref, own, extra, sem,
+    att_out, gq_out, gk_out, gv_out, rows_ref, own, extra, att, sem, att_sem,
 ):
     def block(i):
         return pl.ds(i * BLOCK, BLOCK)
 
+    att_load = pltpu.make_async_copy(att_in, att, att_sem.at[0])
+    att_load.start()
     sides = []
     for side, (near, far) in enumerate(((0, 1), (3, 2))):
         parts = ((gk_out, near, 0), (gv_out, near, 1), (gk_out, far, 2), (gv_out, far, 3))
@@ -491,7 +559,7 @@
         ]
         moved = [
             pltpu.make_async_copy(extra.at[side, slot], out.at[block(near)], sem.at[side, slot])
-            for slot, out in enumerate((gk_out, gv_out, gq_out, att_out))
+            for slot, out in enumerate((gk_out, gv_out, gq_out))
         ]
         added = [
             pltpu.make_async_copy(own.at[side, slot], out.at[block(at)], sem.at[side, slot])
@@ -515,9 +583,14 @@
             part = sum_ref[piece].astype(jnp.float32)[tile * PART : (tile + 1) * PART]
             rows_ref[:, lanes] = part * norm
 
+    att_load.wait()
     for side, ours, theirs, moved, added, away, shared in sides:
         for copy in theirs:
             copy.wait()
+
+        @pl.when(away)
+        def _():
+            att[3 * side * BLOCK : (3 * side + 1) * BLOCK] = extra[side, 3]
 
         @pl.when(away)
         def _():
@@ -532,11 +605,20 @@
                 own[side, slot] = both.astype(jnp.bfloat16)
                 added[slot].start()
 
+    att_store = pltpu.make_async_copy(att, att_out, att_sem.at[0])
+    att_store.start()
     for side, ours, theirs, moved, added, away, shared in sides:
-        @pl.when(jnp.logical_or(away, shared))
+        @pl.when(away)
+        def _():
+            for copy in moved:
+                copy.wait()
+
+        @pl.when(shared)
         def _():
             for copy in added:
                 copy.wait()
+
+    att_store.wait()
 
 
 def on_device(q_tokens, k_tokens, v_tokens, d_attended, w_out, lengths):
@@ -587,7 +669,7 @@
         in_specs=[smem] + [anywhere] * 6,
         out_specs=(anywhere,) * 5 + (smem,),
         scratch_shapes=[slab] * 4 + [square, sides] + [slab] * 4
-        + [sides, pltpu.SMEM((8, 2), jnp.int32), dma((17,))],
+        + [sides, pltpu.SMEM((8, 2), jnp.int32), dma((5,)), dma((2, 4)), dma((4, SLOTS))],
         compiler_params=pltpu.CompilerParams(vmem_limit_bytes=big),
         name="attention",
     )(lengths, q, k, v, dm, halo, w_out)
@@ -602,9 +684,10 @@
         functools.partial(finish_kernel, count),
         out_shape=(halo_shape, sum_shape, token_shape),
         in_specs=[anywhere] * 5,
-        out_specs=(anywhere, vmem, vmem),
+        out_specs=(anywhere, vmem, anywhere),
         scratch_shapes=[
-            slab, slab, square,
+            slab, pltpu.VMEM(mixed_shape.shape[::-1], low), slab, square,
+            pltpu.VMEM((rows, width), low),
             pltpu.VMEM((width, PIECE), jnp.float32),
             pltpu.VMEM((PACKED, 128), jnp.float32),
             pieces(2, SIDE, SIDE), pieces(SIDE, SIDE), pieces(SIDE, SIDE),
@@ -628,9 +711,10 @@
         scratch_shapes=[
             pltpu.VMEM((2, 4, BLOCK, width), low),
             pltpu.VMEM((2, 4, BLOCK, width), low),
-            dma((2, 8)),
+            pltpu.VMEM((rows, width), low),
+            dma((2, 8)), dma((1,)),
         ],
-        input_output_aliases={3: 0, 4: 1, 5: 2, 6: 3},
+        input_output_aliases={4: 1, 5: 2, 6: 3},
         compiler_params=pltpu.CompilerParams(vmem_limit_bytes=big),
         name="settle",
     )(flags, summed, back, att, gq, gk, gv)

time: 105 us -> 103 us (0.981)
  the two profiles are of different devices: /device:TPU:64 before, /device:TPU:34 now
where the time goes in v4:
time: 103 us
  Pallas kernels  102 us (99%)
    pallas_call x1, Pallas kernels, on_device(): pl.pallas_call(functools.partial(finish_kernel, count), out_shape=(halo_s...  51 us
    pallas_call x1, Pallas kernels, on_device(): pl.pallas_call(attention_kernel, out_shape=(mixed_shape, token_shape, tok...  28 us
    pallas_call x1, Pallas kernels, on_device(): pl.pallas_call(functools.partial(exchange_kernel, count), out_shape=(halo...  18 us
    pallas_call x1, Pallas kernels, on_device(): pl.pallas_call(functools.partial(settle_kernel, norm), out_shape=(token_s...  4.75 us

profile of v4, /device:TPU:34, one launch (start us, length us, event | category | flops | bytes accessed | tf_op | source)
XLA Modules:
  0.0 102.5 jit_solution(7285996485765585294)
XLA Ops:
  0.6 18.0 %exchange.1 = (bf16[2,4,128,1152]{3,2,1,0:T(8,128)(2,1)}, bf16[512,1152]{1,0:T(8,128)(2,1)}) custom-call(s32[1,64]{1,0:T(1,128)} %lengths_ref.3, bf16[512,1152]{1,0:T(8,128)(2,1)} %bitcast.8, bf16[512,1152]{1,0:T(8,128)(2,1)} %bitcast.10, bf16[512,1152]{1,0:T(8,128)(2,1)} %bitcast.12, bf16[512,1152]{1,0:T(8,128)(2,1)} %bitcast.14, bf16[1152,1152]{1,0:T(8,128)(2,1)} %w_ref.5), custom_call_target="tpu_custom_call" | custom-call | tf_op jit(solution)/shard_map/exchange/pallas_call | solution.py:637
  18.6 28.0 %attention.1 = (bf16[768,1152]{1,0:T(8,128)(2,1)}, bf16[512,1152]{1,0:T(8,128)(2,1)}, bf16[512,1152]{1,0:T(8,128)(2,1)}, bf16[512,1152]{1,0:T(8,128)(2,1)}, bf16[2,4,128,1152]{3,2,1,0:T(8,128)(2,1)}, /*index=5*/s32[4]{0:T(128)}) custom-call(s32[1,64]{1,0:T(1,128)} %lengths_ref.3, bf16[512,1152]{1,0:T(8,128)(2,1)} %bitcast.9, bf16[512,1152]{1,0:T(8,128)(2,1)} %bitcast.11, ...), custom_call_target="tpu_custom_call" | custom-call | tf_op jit(solution)/shard_map/attention/pallas_call | solution.py:663
  46.6 51.0 %finish.1 = (bf16[2,4,128,1152]{3,2,1,0:T(8,128)(2,1)}, bf16[3,112,128]{2,1,0:T(8,128)(2,1)}, bf16[512,1152]{1,0:T(8,128)(2,1)}) custom-call(bf16[2,4,128,1152]{3,2,1,0:T(8,128)(2,1)} %get-tuple-element.24.ret_ref, bf16[768,1152]{1,0:T(8,128)(2,1)} %get-tuple-element.25.mixed_ref, bf16[512,1152]{1,0:T(8,128)(2,1)} %bitcast.15, ...), custom_call_target="tpu_custom_call" | custom-call | tf_op jit(solution)/shard_map/finish/pallas_call | solution.py:683
  97.6 4.7 %settle.1 = (bf16[512,1152]{1,0:T(8,128)(2,1)}, bf16[512,1152]{1,0:T(8,128)(2,1)}, bf16[512,1152]{1,0:T(8,128)(2,1)}, bf16[512,1152]{1,0:T(8,128)(2,1)}, f32[36,1152]{1,0:T(8,128)}) custom-call(s32[4]{0:T(128)} %get-tuple-element.23.flags_ref, ...), custom_call_target="tpu_custom_call", output_to_operand_aliasing={{1}: (4, {}), {2}: (5, {}), {3}: (6, {})} | custom-call | tf_op jit(solution)/shard_map/settle/pallas_call | solution.py:706

commit v5 on v4

--- a/solution.py
+++ b/solution.py
@@ -32,16 +32,47 @@
     return lax.dot_general(a, b, dims, preferred_element_type=jnp.float32)
 
 
-def boundary(lengths_ref, edge):
+def boundaries(lengths_ref, edges):
     def step(i, carry):
-        start, before, after = carry
+        start, counts = carry
         end = start + lengths_ref[0, i]
-        hit = jnp.logical_and(start < edge, end > edge)
-        return (end, jnp.where(hit, edge - start, before), jnp.where(hit, end - edge, after))
+        new = []
+        for edge, (before, after) in zip(edges, counts):
+            hit = jnp.logical_and(start < edge, end > edge)
+            new.append((jnp.where(hit, edge - start, before), jnp.where(hit, end - edge, after)))
+        return end, tuple(new)
 
     zero = jnp.int32(0)
-    _, before, after = lax.fori_loop(0, lengths_ref.shape[1], step, (zero, zero, zero))
-    return before, after
+    start = (zero, tuple((zero, zero) for _ in edges))
+    return lax.fori_loop(0, lengths_ref.shape[1], step, start)[1]
+
+
+def plans(lengths_ref, first):
+    counts = boundaries(lengths_ref, [first - OWN, first, first + OWN, first + 2 * OWN])
+
+    def is_pair(pair, before, after):
+        return jnp.logical_and(pair[0] == before, pair[1] == after)
+
+    result = []
+    for at in (1, 2):
+        here = counts[at]
+        left_full = is_pair(counts[at - 1], 1, 3)
+        right_full = is_pair(counts[at + 1], 3, 1)
+        only_left = jnp.logical_and(left_full, jnp.logical_not(right_full))
+        only_right = jnp.logical_and(right_full, jnp.logical_not(left_full))
+        to_left = (
+            is_pair(here, 3, 1)
+            | (is_pair(here, 2, 1) & right_full)
+            | (is_pair(here, 1, 1) & only_right)
+        )
+        to_right = (
+            is_pair(here, 1, 3)
+            | (is_pair(here, 1, 2) & left_full)
+            | (is_pair(here, 1, 1) & only_left)
+        )
+        shared = (here[0] > 0) & jnp.logical_not(to_left | to_right)
+        result.append((here[0], here[1], to_left, to_right, shared))
+    return result
 
 
 def greet(others):
@@ -101,9 +132,9 @@
         send(side, 1, v_ref.at[near[side]])
     for load in loads[:-1]:
         load.wait()
+    edges = plans(lengths_ref, first)
     for side in range(2):
-        before, after = boundary(lengths_ref, first + side * OWN)
-        shared = jnp.logical_and(before == 2, after == 2)
+        shared = edges[side][-1]
         pack[side, 0] = jnp.where(shared, far_buf[side, 0], near_buf[side])
         pack[side, 1] = jnp.where(shared, far_buf[side, 1], dy_buf[near[side]])
         send(side, 2, pack.at[side, 0])
@@ -180,15 +211,13 @@
     for load in loads:
         load.start()
 
-    l_before, l_after = boundary(lengths_ref, first)
-    r_before, r_after = boundary(lengths_ref, last)
-    l_shared = jnp.logical_and(l_before == 2, l_after == 2)
-    r_shared = jnp.logical_and(r_before == 2, r_after == 2)
-    l_away = l_after == 1
-    l_here = jnp.logical_and(l_before == 1, l_after > 1)
-    r_here = r_after == 1
-    r_away = jnp.logical_and(r_before == 1, r_after > 1)
-    for i, flag in enumerate((l_away, l_shared, r_away, r_shared)):
+    left_edge, right_edge = plans(lengths_ref, first)
+    l_before, l_after, l_away, l_here, l_shared = left_edge
+    r_before, r_after, r_here, r_away, r_shared = right_edge
+    flags = (
+        l_away, l_shared, l_shared & (l_after == 2), r_away, r_shared, r_shared & (r_before == 2)
+    )
+    for i, flag in enumerate(flags):
         flags_out[i] = flag.astype(jnp.int32)
 
     halo_loads = []
@@ -216,21 +245,20 @@
         on_left = jnp.logical_and(start < first, end > first)
         on_right = jnp.logical_and(start < last, end > last)
         within = jnp.logical_and(start >= first, end <= last)
-        mine = jnp.logical_or(
-            within,
-            jnp.logical_or(
-                jnp.logical_and(on_left, jnp.logical_not(l_away)),
-                jnp.logical_and(on_right, jnp.logical_not(r_away)),
-            ),
-        )
-        shared = jnp.logical_or(
-            jnp.logical_and(on_left, l_shared), jnp.logical_and(on_right, r_shared)
-        )
+        mine = (
+            within
+            | (on_left & jnp.logical_not(l_away))
+            | (on_right & jnp.logical_not(r_away))
+        )
+        shared = (on_left & l_shared) | (on_right & r_shared)
+        own_blocks = jnp.where(on_left, l_after, r_before)
 
         @pl.when(mine)
         def _():
-            work[number, 0] = jnp.where(shared, 5, end - start)
-            work[number, 1] = start - first + 2
+            k_at = start - first + 2
+            work[number, 0] = jnp.where(shared, own_blocks * 8 + end - start, end - start)
+            work[number, 1] = jnp.where(shared & on_left, 2, k_at)
+            work[number, 2] = k_at
 
         return end, number + mine.astype(jnp.int32)
 
@@ -276,20 +304,13 @@
                     store(index, slot).start()
 
     def image(i, carry):
-        kind, at = work[i, 0], work[i, 1]
-        for blocks in range(1, OWN + 1):
-            @pl.when(kind == blocks)
+        kind, q_at, k_at = work[i, 0], work[i, 1], work[i, 2]
+        for q_blocks, k_blocks in ((1, 1), (2, 2), (3, 3), (4, 4), (1, 2), (1, 3), (2, 3), (2, 4)):
+            @pl.when(kind == (k_blocks if q_blocks == k_blocks else q_blocks * 8 + k_blocks))
             def _():
-                attend(*bufs, at, blocks, at, blocks)
-                for j in range(blocks):
-                    store_all(at + j, range(4))
-
-        @pl.when(kind == 5)
-        def _():
-            q_at = jnp.where(at == 0, 2, 4)
-            attend(*bufs, q_at, 2, at, 4)
-            for j in range(2):
-                store_all(q_at + j, range(4))
+                attend(*bufs, q_at, q_blocks, k_at, k_blocks)
+                for j in range(q_blocks):
+                    store_all(q_at + j, range(4))
 
         return carry
 
@@ -393,6 +414,9 @@
         turned_mixed[lanes] = mixed[:, lanes].T
     stage[...] = jnp.zeros_like(stage)
 
+    def x_first(piece, on_core_0):
+        return on_core_0 if piece < PIECES - 1 else False
+
     def product(piece):
         columns = slice(piece * PIECE, (piece + 1) * PIECE)
 
@@ -404,7 +428,7 @@
         lax.fori_loop(0, D // PIECE, weight, 0)
         for part in range(D // PART):
             px, pz, pcore = part // 8, part // 2 % 4, part % 2
-            place = (pz, px) if pcore else (px, pz)
+            place = (px, pz) if x_first(piece, pcore == 0) else (pz, px)
             for tile in range(PIECE // 128):
                 stage[tile * PART : (tile + 1) * PART] = acc[
                     part * PART : (part + 1) * PART, tile * 128 : (tile + 1) * 128
@@ -441,14 +465,14 @@
         one[piece].wait_recv()
         for row in range(SIDE):
             total[piece, row] = add(parts[piece, core, row], sibling[piece, row])
-        twos.append(spread(0, piece, total.at[piece], second.at[piece], core == 0))
+        twos.append(spread(0, piece, total.at[piece], second.at[piece], x_first(piece, core == 0)))
 
     def third_stage(piece):
         at, started = twos[piece]
         for copy in started:
             copy.wait_recv()
         half[piece] = add(total[piece, at], *[second[piece, step - 1] for step in steps])
-        threes.append(spread(1, piece, half.at[piece], third.at[piece], core == 1))
+        threes.append(spread(1, piece, half.at[piece], third.at[piece], jnp.logical_not(x_first(piece, core == 0))))
 
     product(0)
     meet(others)
@@ -565,10 +589,10 @@
             pltpu.make_async_copy(own.at[side, slot], out.at[block(at)], sem.at[side, slot])
             for out, at, slot in parts
         ]
-        away, shared = flags_ref[2 * side] == 1, flags_ref[2 * side + 1] == 1
-        sides.append((side, ours, theirs, moved, added, away, shared))
-
-    for side, ours, theirs, moved, added, away, shared in sides:
+        away, shared, both = (flags_ref[3 * side + i] == 1 for i in range(3))
+        sides.append((side, ours, theirs, moved, added, away, shared, both))
+
+    for side, ours, theirs, moved, added, away, shared, both in sides:
         for copy in theirs:
             copy.start()
 
@@ -584,7 +608,7 @@
             rows_ref[:, lanes] = part * norm
 
     att_load.wait()
-    for side, ours, theirs, moved, added, away, shared in sides:
+    for side, ours, theirs, moved, added, away, shared, both in sides:
         for copy in theirs:
             copy.wait()
 
@@ -601,13 +625,16 @@
         def _():
             for slot in range(4):
                 ours[slot].wait()
-                both = own[side, slot].astype(jnp.float32) + extra[side, slot].astype(jnp.float32)
-                own[side, slot] = both.astype(jnp.bfloat16)
+                total = own[side, slot].astype(jnp.float32)
+                other = extra[side, slot].astype(jnp.float32)
+                if slot >= 2:
+                    other = jnp.where(both, other, 0.0)
+                own[side, slot] = (total + other).astype(jnp.bfloat16)
                 added[slot].start()
 
     att_store = pltpu.make_async_copy(att, att_out, att_sem.at[0])
     att_store.start()
-    for side, ours, theirs, moved, added, away, shared in sides:
+    for side, ours, theirs, moved, added, away, shared, both in sides:
         @pl.when(away)
         def _():
             for copy in moved:
@@ -664,12 +691,12 @@
         attention_kernel,
         out_shape=(
             mixed_shape, token_shape, token_shape, token_shape, halo_shape,
-            jax.ShapeDtypeStruct((4,), jnp.int32),
+            jax.ShapeDtypeStruct((6,), jnp.int32),
         ),
         in_specs=[smem] + [anywhere] * 6,
         out_specs=(anywhere,) * 5 + (smem,),
         scratch_shapes=[slab] * 4 + [square, sides] + [slab] * 4
-        + [sides, pltpu.SMEM((8, 2), jnp.int32), dma((5,)), dma((2, 4)), dma((4, SLOTS))],
+        + [sides, pltpu.SMEM((8, 3), jnp.int32), dma((5,)), dma((2, 4)), dma((4, SLOTS))],
         compiler_params=pltpu.CompilerParams(vmem_limit_bytes=big),
         name="attention",
     )(lengths, q, k, v, dm, halo, w_out)

time: 103 us -> 96.9 us (0.941)
  the two profiles are of different devices: /device:TPU:34 before, /device:TPU:64 now
where the time goes in v5:
time: 96.9 us; the launch traced here: 96.7 us
  Pallas kernels  95.9 us (99%)
    pallas_call x1, Pallas kernels, on_device(): pl.pallas_call(functools.partial(finish_kernel, count), out_shape=(halo_s...  42.1 us
    pallas_call x1, Pallas kernels, on_device(): pl.pallas_call(attention_kernel, out_shape=(mixed_shape, token_shape, tok...  29.6 us
    pallas_call x1, Pallas kernels, on_device(): pl.pallas_call(functools.partial(exchange_kernel, count), out_shape=(halo...  18 us
    pallas_call x1, Pallas kernels, on_device(): pl.pallas_call(functools.partial(settle_kernel, norm), out_shape=(token_s...  6.21 us

profile of v5, /device:TPU:64, one launch (start us, length us, event | category | flops | bytes accessed | tf_op | source)
XLA Modules:
  0.0 96.7 jit_solution(13433289397500508552)
XLA Ops:
  0.6 18.0 %exchange.1 = (bf16[2,4,128,1152]{3,2,1,0:T(8,128)(2,1)}, bf16[512,1152]{1,0:T(8,128)(2,1)}) custom-call(s32[1,64]{1,0:T(1,128)} %lengths_ref.3, bf16[512,1152]{1,0:T(8,128)(2,1)} %bitcast.8, bf16[512,1152]{1,0:T(8,128)(2,1)} %bitcast.10, bf16[512,1152]{1,0:T(8,128)(2,1)} %bitcast.12, bf16[512,1152]{1,0:T(8,128)(2,1)} %bitcast.14, bf16[1152,1152]{1,0:T(8,128)(2,1)} %w_ref.5), custom_call_target="tpu_custom_call" | custom-call | tf_op jit(solution)/shard_map/exchange/pallas_call | solution.py:664
  18.6 29.6 %attention.1 = (bf16[768,1152]{1,0:T(8,128)(2,1)}, bf16[512,1152]{1,0:T(8,128)(2,1)}, bf16[512,1152]{1,0:T(8,128)(2,1)}, bf16[512,1152]{1,0:T(8,128)(2,1)}, bf16[2,4,128,1152]{3,2,1,0:T(8,128)(2,1)}, /*index=5*/s32[6]{0:T(128)}) custom-call(s32[1,64]{1,0:T(1,128)} %lengths_ref.3, bf16[512,1152]{1,0:T(8,128)(2,1)} %bitcast.9, bf16[512,1152]{1,0:T(8,128)(2,1)} %bitcast.11, ...), custom_call_target="tpu_custom_call" | custom-call | tf_op jit(solution)/shard_map/attention/pallas_call | solution.py:690
  48.2 42.1 %finish.1 = (bf16[2,4,128,1152]{3,2,1,0:T(8,128)(2,1)}, bf16[3,112,128]{2,1,0:T(8,128)(2,1)}, bf16[512,1152]{1,0:T(8,128)(2,1)}) custom-call(bf16[2,4,128,1152]{3,2,1,0:T(8,128)(2,1)} %get-tuple-element.24.ret_ref, bf16[768,1152]{1,0:T(8,128)(2,1)} %get-tuple-element.25.mixed_ref, bf16[512,1152]{1,0:T(8,128)(2,1)} %bitcast.15, ...), custom_call_target="tpu_custom_call" | custom-call | tf_op jit(solution)/shard_map/finish/pallas_call | solution.py:710
  90.3 6.2 %settle.1 = (bf16[512,1152]{1,0:T(8,128)(2,1)}, bf16[512,1152]{1,0:T(8,128)(2,1)}, bf16[512,1152]{1,0:T(8,128)(2,1)}, bf16[512,1152]{1,0:T(8,128)(2,1)}, f32[36,1152]{1,0:T(8,128)}) custom-call(s32[6]{0:T(128)} %get-tuple-element.23.flags_ref, ...), custom_call_target="tpu_custom_call", output_to_operand_aliasing={{1}: (4, {}), {2}: (5, {}), {3}: (6, {})} | custom-call | tf_op jit(solution)/shard_map/settle/pallas_call | solution.py:733

commit v6 on v5

--- a/solution.py
+++ b/solution.py
@@ -364,7 +364,7 @@
 def finish_kernel(
     count, ret_ref, mixed_ref, dy_ref, halo_ref, w_ref, back_ref, sum_ref, att_ref,
     mixed, turned_mixed, dy, w_buf, att, acc, stage, parts, sibling, total, second, half, third, whole, fourth, fifth,
-    load_sem, ret_send, ret_recv, one_send, one_recv, sends, recvs,
+    load_sem, ret_send, ret_recv, one_send, one_recv, sends, recvs, relay, relay_send, relay_recv,
 ):
     left, right = ring_neighbours(count)
     me, y = lax.axis_index("tok"), lax.axis_index("dp")
@@ -391,7 +391,32 @@
     along_x = [device(turned(x, step), y, z, core) for step in steps]
     along_y = [device(x, turned(y, step), z, core) for step in steps]
     along_z = [device(x, y, turned(z, step), core) for step in steps]
-    others = [left, right, other] + along_x + along_y + along_z
+    across = [device(turned(x, step), y, z, 1 - core) for step in (1, SIDE - 1)]
+    others = [left, right, other] + across + along_x + along_y + along_z
+    at_end = (z == 0) | (z == SIDE - 1)
+    crosses = at_end & ((core == 1) == (z == SIDE - 1))
+    forwards = at_end & jnp.logical_not(crosses)
+    opposite = device(x, y, SIDE - 1 - z, core)
+    beyond = device(turned(x, jnp.where(core == 1, 1, SIDE - 1)), y, z, 1 - core)
+
+    def to_forwarder(slot):
+        return remote(
+            ret_ref.at[core, 2 + slot], relay.at[slot], relay_send.at[slot], relay_recv.at[slot],
+            opposite,
+        )
+
+    def forward(slot):
+        return remote(
+            relay.at[slot], back_ref.at[1 - core, 2 + slot],
+            relay_send.at[slot], ret_recv.at[1 - core, 2 + slot], beyond,
+        )
+
+    def pass_on(slot):
+        @pl.when(forwards)
+        def _():
+            to_forwarder(slot).wait_recv()
+            forward(slot).start()
+
     greet(others)
     copies = []
 
@@ -477,19 +502,32 @@
     product(0)
     meet(others)
     one = [to_sibling(0)]
+    @pl.when(crosses)
+    def _():
+        for slot in range(2):
+            to_forwarder(slot).start()
+
     returns = []
     for side in range(2):
         for slot in range(4):
-            returns.append(send(
+            copy = remote(
                 ret_ref.at[side, slot], back_ref.at[1 - side, slot],
                 ret_send.at[side, slot], ret_recv.at[1 - side, slot],
                 {"tok": right if side else left},
-            ))
+            )
+            direct = True if slot < 2 else jnp.logical_not(crosses & (core == side))
+            returns.append((copy, direct))
+
+            @pl.when(direct)
+            def _():
+                copy.start()
+
     for piece in range(1, PIECES):
         product(piece)
         one.append(to_sibling(piece))
         second_stage(piece - 1)
     second_stage(PIECES - 1)
+    pass_on(0)
 
     loads[-1].wait()
     for part in range(OWN):
@@ -500,6 +538,7 @@
     att_store.start()
     for piece in range(PIECES):
         third_stage(piece)
+    pass_on(1)
 
     gap = lax.rem(z - y + SIDE, SIDE)
 
@@ -552,8 +591,23 @@
             def _():
                 to_plane(piece, step).wait_send()
 
-    for copy in returns:
+    for copy, direct in returns:
         copy.wait_recv()
+
+        @pl.when(direct)
+        def _():
+            copy.wait_send()
+
+    @pl.when(crosses)
+    def _():
+        for slot in range(2):
+            to_forwarder(slot).wait_send()
+
+    @pl.when(forwards)
+    def _():
+        for slot in range(2):
+            forward(slot).wait_send()
+
     for copy in copies:
         copy.wait_send()
     att_store.wait()
@@ -723,6 +777,7 @@
             pltpu.VMEM((2, PIECES, PACKED, 128), low),
             dma((5,)), dma((2, 4)), dma((2, 4)), dma((PIECES,)), dma((PIECES,)),
             dma((4, PIECES, SIDE - 1)), dma((4, PIECES, SIDE - 1)),
+            sides, dma((2,)), dma((2,)),
         ],
         compiler_params=pltpu.CompilerParams(
             collective_id=1, has_side_effects=True, vmem_limit_bytes=big

time: 96.9 us -> 90.8 us (0.937)
  Pallas kernels: 95.9 us -> 89.8 us
    pallas_call x1, Pallas kernels: 29.6 us -> 19.9 us  [on_device(): pl.pallas_call(attention_kernel, out_shape=(mixed_shape, token_shape, tok...]
    pallas_call x1, Pallas kernels: 42.1 us -> 46.3 us  [on_device(): pl.pallas_call(functools.partial(finish_kernel, count), out_shape=(halo_s...]
where the time goes in v6:
time: 90.8 us; the launch traced here: 90.6 us
  Pallas kernels  89.8 us (99%)
    pallas_call x1, Pallas kernels, on_device(): pl.pallas_call(functools.partial(finish_kernel, count), out_shape=(halo_s...  46.3 us
    pallas_call x1, Pallas kernels, on_device(): pl.pallas_call(attention_kernel, out_shape=(mixed_shape, token_shape, tok...  19.9 us
    pallas_call x1, Pallas kernels, on_device(): pl.pallas_call(functools.partial(exchange_kernel, count), out_shape=(halo...  18 us
    pallas_call x1, Pallas kernels, on_device(): pl.pallas_call(functools.partial(settle_kernel, norm), out_shape=(token_s...  5.55 us

profile of v6, /device:TPU:64, one launch (start us, length us, event | category | flops | bytes accessed | tf_op | source)
XLA Modules:
  0.0 90.6 jit_solution(213400323605101050)
XLA Ops:
  0.6 18.0 %exchange.1 = (bf16[2,4,128,1152]{3,2,1,0:T(8,128)(2,1)}, bf16[512,1152]{1,0:T(8,128)(2,1)}) custom-call(s32[1,64]{1,0:T(1,128)} %lengths_ref.3, bf16[512,1152]{1,0:T(8,128)(2,1)} %bitcast.8, bf16[512,1152]{1,0:T(8,128)(2,1)} %bitcast.10, bf16[512,1152]{1,0:T(8,128)(2,1)} %bitcast.12, bf16[512,1152]{1,0:T(8,128)(2,1)} %bitcast.14, bf16[1152,1152]{1,0:T(8,128)(2,1)} %w_ref.5), custom_call_target="tpu_custom_call" | custom-call | tf_op jit(solution)/shard_map/exchange/pallas_call | solution.py:718
  18.6 19.9 %attention.1 = (bf16[768,1152]{1,0:T(8,128)(2,1)}, bf16[512,1152]{1,0:T(8,128)(2,1)}, bf16[512,1152]{1,0:T(8,128)(2,1)}, bf16[512,1152]{1,0:T(8,128)(2,1)}, bf16[2,4,128,1152]{3,2,1,0:T(8,128)(2,1)}, /*index=5*/s32[6]{0:T(128)}) custom-call(s32[1,64]{1,0:T(1,128)} %lengths_ref.3, bf16[512,1152]{1,0:T(8,128)(2,1)} %bitcast.9, bf16[512,1152]{1,0:T(8,128)(2,1)} %bitcast.11, ...), custom_call_target="tpu_custom_call" | custom-call | tf_op jit(solution)/shard_map/attention/pallas_call | solution.py:744
  38.6 46.3 %finish.1 = (bf16[2,4,128,1152]{3,2,1,0:T(8,128)(2,1)}, bf16[3,112,128]{2,1,0:T(8,128)(2,1)}, bf16[512,1152]{1,0:T(8,128)(2,1)}) custom-call(bf16[2,4,128,1152]{3,2,1,0:T(8,128)(2,1)} %get-tuple-element.24.ret_ref, bf16[768,1152]{1,0:T(8,128)(2,1)} %get-tuple-element.25.mixed_ref, bf16[512,1152]{1,0:T(8,128)(2,1)} %bitcast.15, ...), custom_call_target="tpu_custom_call" | custom-call | tf_op jit(solution)/shard_map/finish/pallas_call | solution.py:764
  84.9 5.6 %settle.1 = (bf16[512,1152]{1,0:T(8,128)(2,1)}, bf16[512,1152]{1,0:T(8,128)(2,1)}, bf16[512,1152]{1,0:T(8,128)(2,1)}, bf16[512,1152]{1,0:T(8,128)(2,1)}, f32[36,1152]{1,0:T(8,128)}) custom-call(s32[6]{0:T(128)} %get-tuple-element.23.flags_ref, ...), custom_call_target="tpu_custom_call", output_to_operand_aliasing={{1}: (4, {}), {2}: (5, {}), {3}: (6, {})} | custom-call | tf_op jit(solution)/shard_map/settle/pallas_call | solution.py:788

commit v7 on v6

--- a/solution.py
+++ b/solution.py
@@ -94,7 +94,7 @@
 
 def exchange_kernel(
     count, lengths_ref, q_ref, k_ref, v_ref, dy_ref, w_ref, halo_ref, dm_ref,
-    dy_buf, w_buf, near_buf, far_buf, pack, load_sem, send_sem, recv_sem,
+    dy_buf, w_buf, near_buf, far_buf, pack, dm_buf, load_sem, send_sem, recv_sem,
 ):
     left, right = ring_neighbours(count)
     first = lax.axis_index("tok") * OWN
@@ -142,9 +142,12 @@
     loads[-1].wait()
     for part in range(OWN):
         rows = slice(part * BLOCK, (part + 1) * BLOCK)
-        dm_ref[rows] = dot(dy_buf[rows], w_buf[...], NT).astype(jnp.bfloat16)
+        dm_buf[rows] = dot(dy_buf[rows], w_buf[...], NT).astype(jnp.bfloat16)
+    dm_store = pltpu.make_async_copy(dm_buf, dm_ref, load_sem.at[0])
+    dm_store.start()
     for copy in copies:
         copy.wait()
+    dm_store.wait()
 
 
 def attend(q_buf, k_buf, v_buf, dm_buf, mixed, gq, gk, gv, q_at, q_blocks, k_at, k_blocks):
@@ -204,10 +207,13 @@
 
     loads = [
         (q_ref, q_buf.at[own]), (k_ref, k_buf.at[own]), (v_ref, v_buf.at[own]),
-        (dm_ref, dm_buf.at[own]), (w_ref, w_buf),
+        (dm_ref, dm_buf.at[own]),
     ]
+    for i in range(4):
+        part = pl.ds(i * (D // 4), D // 4)
+        loads.append((w_ref.at[part], w_buf.at[part]))
     loads = [pltpu.make_async_copy(a, b, sem.at[i]) for i, (a, b) in enumerate(loads)]
-    w_load = loads.pop()
+    loads, w_loads = loads[:4], loads[4:]
     for load in loads:
         load.start()
 
@@ -237,7 +243,8 @@
             for load in some:
                 load.start()
 
-    w_load.start()
+    for load in w_loads:
+        load.start()
 
     def collect(i, carry):
         start, number = carry
@@ -273,7 +280,11 @@
             for load in some:
                 load.wait()
 
-    w_load.wait()
+    @pl.when(l_here | r_here)
+    def _():
+        for load in w_loads:
+            load.wait()
+
     for side, (here, slot) in enumerate(((l_here, 1), (r_here, 6))):
         @pl.when(here)
         def _():
@@ -355,6 +366,11 @@
             for copy in some:
                 copy.wait()
 
+    @pl.when(jnp.logical_not(l_here | r_here))
+    def _():
+        for load in w_loads:
+            load.wait()
+
     for slot in range(1, 3 + OWN):
         for index in range(4):
             if index == 0 or 2 <= slot < 2 + OWN:
@@ -369,10 +385,15 @@
     left, right = ring_neighbours(count)
     me, y = lax.axis_index("tok"), lax.axis_index("dp")
     core, z, x = lax.rem(me, 2), lax.rem(me // 2, SIDE), me // (2 * SIDE)
-    loads = [
-        (mixed_ref, mixed),
+    loads = []
+    for i in range(OWN + 2):
+        part = pl.ds(i * BLOCK, BLOCK)
+        loads.append((mixed_ref.at[part], mixed.at[part]))
+    for i in range(2):
+        part = i * 2 * BLOCK
+        loads.append((dy_ref.at[pl.ds(part, 2 * BLOCK)], dy.at[pl.ds(part + BLOCK, 2 * BLOCK)]))
+    loads += [
         (halo_ref.at[0, 3], dy.at[pl.ds(0, BLOCK)]),
-        (dy_ref, dy.at[pl.ds(BLOCK, OWN * BLOCK)]),
         (halo_ref.at[1, 3], dy.at[pl.ds((OWN + 1) * BLOCK, BLOCK)]),
         (w_ref, w_buf),
     ]
@@ -515,10 +536,10 @@
                 ret_send.at[side, slot], ret_recv.at[1 - side, slot],
                 {"tok": right if side else left},
             )
-            direct = True if slot < 2 else jnp.logical_not(crosses & (core == side))
-            returns.append((copy, direct))
-
-            @pl.when(direct)
+            over_x = crosses & (core == side)
+            returns.append((copy, over_x, slot))
+
+            @pl.when(jnp.logical_not(over_x))
             def _():
                 copy.start()
 
@@ -527,7 +548,11 @@
         one.append(to_sibling(piece))
         second_stage(piece - 1)
     second_stage(PIECES - 1)
-    pass_on(0)
+    for copy, over_x, slot in returns:
+        if slot < 2:
+            @pl.when(over_x)
+            def _():
+                copy.start()
 
     loads[-1].wait()
     for part in range(OWN):
@@ -538,6 +563,7 @@
     att_store.start()
     for piece in range(PIECES):
         third_stage(piece)
+    pass_on(0)
     pass_on(1)
 
     gap = lax.rem(z - y + SIDE, SIDE)
@@ -591,10 +617,10 @@
             def _():
                 to_plane(piece, step).wait_send()
 
-    for copy, direct in returns:
+    for copy, over_x, slot in returns:
         copy.wait_recv()
 
-        @pl.when(direct)
+        @pl.when(True if slot < 2 else jnp.logical_not(over_x))
         def _():
             copy.wait_send()
 
@@ -620,8 +646,16 @@
     def block(i):
         return pl.ds(i * BLOCK, BLOCK)
 
-    att_load = pltpu.make_async_copy(att_in, att, att_sem.at[0])
-    att_load.start()
+    att_loads = [
+        pltpu.make_async_copy(att_in.at[block(i)], att.at[block(i)], att_sem.at[i])
+        for i in range(OWN)
+    ]
+    att_stores = [
+        pltpu.make_async_copy(att.at[block(i)], att_out.at[block(i)], att_sem.at[i])
+        for i in range(OWN)
+    ]
+    for copy in att_loads:
+        copy.start()
     sides = []
     for side, (near, far) in enumerate(((0, 1), (3, 2))):
         parts = ((gk_out, near, 0), (gv_out, near, 1), (gk_out, far, 2), (gv_out, far, 3))
@@ -647,8 +681,10 @@
         sides.append((side, ours, theirs, moved, added, away, shared, both))
 
     for side, ours, theirs, moved, added, away, shared, both in sides:
-        for copy in theirs:
-            copy.start()
+        @pl.when(jnp.logical_or(away, shared))
+        def _():
+            for copy in theirs:
+                copy.start()
 
         @pl.when(shared)
         def _():
@@ -661,14 +697,20 @@
             part = sum_ref[piece].astype(jnp.float32)[tile * PART : (tile + 1) * PART]
             rows_ref[:, lanes] = part * norm
 
-    att_load.wait()
+    for copy in att_loads:
+        copy.wait()
     for side, ours, theirs, moved, added, away, shared, both in sides:
-        for copy in theirs:
-            copy.wait()
+        @pl.when(jnp.logical_or(away, shared))
+        def _():
+            for copy in theirs:
+                copy.wait()
 
         @pl.when(away)
         def _():
             att[3 * side * BLOCK : (3 * side + 1) * BLOCK] = extra[side, 3]
+
+        att_stores[3 * side].start()
+        att_stores[1 + side].start()
 
         @pl.when(away)
         def _():
@@ -686,8 +728,6 @@
                 own[side, slot] = (total + other).astype(jnp.bfloat16)
                 added[slot].start()
 
-    att_store = pltpu.make_async_copy(att, att_out, att_sem.at[0])
-    att_store.start()
     for side, ours, theirs, moved, added, away, shared, both in sides:
         @pl.when(away)
         def _():
@@ -699,7 +739,8 @@
             for copy in added:
                 copy.wait()
 
-    att_store.wait()
+    for copy in att_stores:
+        copy.wait()
 
 
 def on_device(q_tokens, k_tokens, v_tokens, d_attended, w_out, lengths):
@@ -719,13 +760,14 @@
         functools.partial(exchange_kernel, count),
         out_shape=(halo_shape, token_shape),
         in_specs=[smem] + [anywhere] * 5,
-        out_specs=(anywhere, vmem),
+        out_specs=(anywhere, anywhere),
         scratch_shapes=[
             pltpu.VMEM((rows, width), low),
             pltpu.VMEM((width, width), low),
             pltpu.VMEM((2, BLOCK, width), low),
             pltpu.VMEM((2, 2, BLOCK, width), low),
             pltpu.VMEM((2, 2, BLOCK, width), low),
+            pltpu.VMEM((rows, width), low),
             pltpu.SemaphoreType.DMA((8,)),
             pltpu.SemaphoreType.DMA((2, 4)),
             pltpu.SemaphoreType.DMA((2, 4)),
@@ -750,7 +792,7 @@
         in_specs=[smem] + [anywhere] * 6,
         out_specs=(anywhere,) * 5 + (smem,),
         scratch_shapes=[slab] * 4 + [square, sides] + [slab] * 4
-        + [sides, pltpu.SMEM((8, 3), jnp.int32), dma((5,)), dma((2, 4)), dma((4, SLOTS))],
+        + [sides, pltpu.SMEM((8, 3), jnp.int32), dma((8,)), dma((2, 4)), dma((4, SLOTS))],
         compiler_params=pltpu.CompilerParams(vmem_limit_bytes=big),
         name="attention",
     )(lengths, q, k, v, dm, halo, w_out)
@@ -775,7 +817,7 @@
             pieces(SIDE - 1, SIDE), pieces(SIDE), pieces(SIDE - 1),
             pieces(), pieces(SIDE - 1),
             pltpu.VMEM((2, PIECES, PACKED, 128), low),
-            dma((5,)), dma((2, 4)), dma((2, 4)), dma((PIECES,)), dma((PIECES,)),
+            dma((11,)), dma((2, 4)), dma((2, 4)), dma((PIECES,)), dma((PIECES,)),
             dma((4, PIECES, SIDE - 1)), dma((4, PIECES, SIDE - 1)),
             sides, dma((2,)), dma((2,)),
         ],
@@ -794,7 +836,7 @@
             pltpu.VMEM((2, 4, BLOCK, width), low),
             pltpu.VMEM((2, 4, BLOCK, width), low),
             pltpu.VMEM((rows, width), low),
-            dma((2, 8)), dma((1,)),
+            dma((2, 8)), dma((OWN,)),
         ],
         input_output_aliases={4: 1, 5: 2, 6: 3},
         compiler_params=pltpu.CompilerParams(vmem_limit_bytes=big),

time: 90.8 us -> 87.4 us (0.963)
  Pallas kernels: 89.8 us -> 86.4 us
    pallas_call x1, Pallas kernels: 46.3 us -> 39.8 us  [on_device(): pl.pallas_call(functools.partial(finish_kernel, count), out_shape=(halo_s...]
    pallas_call x1, Pallas kernels: 19.9 us -> 23.6 us  [on_device(): pl.pallas_call(attention_kernel, out_shape=(mixed_shape, token_shape, tok...]
    pallas_call x1, Pallas kernels: 18 us -> 16.9 us  [on_device(): pl.pallas_call(functools.partial(exchange_kernel, count), out_shape=(halo...]
where the time goes in v7:
time: 87.4 us; the launch traced here: 87.2 us
  Pallas kernels  86.4 us (99%)
    pallas_call x1, Pallas kernels, on_device(): pl.pallas_call(functools.partial(finish_kernel, count), out_shape=(halo_s...  39.8 us
    pallas_call x1, Pallas kernels, on_device(): pl.pallas_call(attention_kernel, out_shape=(mixed_shape, token_shape, tok...  23.6 us
    pallas_call x1, Pallas kernels, on_device(): pl.pallas_call(functools.partial(exchange_kernel, count), out_shape=(halo...  16.9 us
    pallas_call x1, Pallas kernels, on_device(): pl.pallas_call(functools.partial(settle_kernel, norm), out_shape=(token_s...  6.11 us

profile of v7, /device:TPU:64, one launch (start us, length us, event | category | flops | bytes accessed | tf_op | source)
XLA Modules:
  0.0 87.2 jit_solution(10408107127013496023)
XLA Ops:
  0.6 16.9 %exchange.1 = (bf16[2,4,128,1152]{3,2,1,0:T(8,128)(2,1)}, bf16[512,1152]{1,0:T(8,128)(2,1)}) custom-call(s32[1,64]{1,0:T(1,128)} %lengths_ref.3, bf16[512,1152]{1,0:T(8,128)(2,1)} %bitcast.8, bf16[512,1152]{1,0:T(8,128)(2,1)} %bitcast.10, bf16[512,1152]{1,0:T(8,128)(2,1)} %bitcast.12, bf16[512,1152]{1,0:T(8,128)(2,1)} %bitcast.14, bf16[1152,1152]{1,0:T(8,128)(2,1)} %w_ref.5), custom_call_target="tpu_custom_call" | custom-call | tf_op jit(solution)/shard_map/exchange/pallas_call | solution.py:759
  17.6 23.6 %attention.1 = (bf16[768,1152]{1,0:T(8,128)(2,1)}, bf16[512,1152]{1,0:T(8,128)(2,1)}, bf16[512,1152]{1,0:T(8,128)(2,1)}, bf16[512,1152]{1,0:T(8,128)(2,1)}, bf16[2,4,128,1152]{3,2,1,0:T(8,128)(2,1)}, /*index=5*/s32[6]{0:T(128)}) custom-call(s32[1,64]{1,0:T(1,128)} %lengths_ref.3, bf16[512,1152]{1,0:T(8,128)(2,1)} %bitcast.9, bf16[512,1152]{1,0:T(8,128)(2,1)} %bitcast.11, ...), custom_call_target="tpu_custom_call" | custom-call | tf_op jit(solution)/shard_map/attention/pallas_call | solution.py:786
  41.2 39.8 %finish.1 = (bf16[2,4,128,1152]{3,2,1,0:T(8,128)(2,1)}, bf16[3,112,128]{2,1,0:T(8,128)(2,1)}, bf16[512,1152]{1,0:T(8,128)(2,1)}) custom-call(bf16[2,4,128,1152]{3,2,1,0:T(8,128)(2,1)} %get-tuple-element.24.ret_ref, bf16[768,1152]{1,0:T(8,128)(2,1)} %get-tuple-element.25.mixed_ref, bf16[512,1152]{1,0:T(8,128)(2,1)} %bitcast.15, ...), custom_call_target="tpu_custom_call" | custom-call | tf_op jit(solution)/shard_map/finish/pallas_call | solution.py:806
  81.0 6.1 %settle.1 = (bf16[512,1152]{1,0:T(8,128)(2,1)}, bf16[512,1152]{1,0:T(8,128)(2,1)}, bf16[512,1152]{1,0:T(8,128)(2,1)}, bf16[512,1152]{1,0:T(8,128)(2,1)}, f32[36,1152]{1,0:T(8,128)}) custom-call(s32[6]{0:T(128)} %get-tuple-element.23.flags_ref, ...), custom_call_target="tpu_custom_call", output_to_operand_aliasing={{1}: (4, {}), {2}: (5, {}), {3}: (6, {})} | custom-call | tf_op jit(solution)/shard_map/settle/pallas_call | solution.py:830

commit v8 on v7

--- a/solution.py
+++ b/solution.py
@@ -155,7 +155,7 @@
     k_rows = pl.ds(pl.multiple_of(k_at * BLOCK, BLOCK), k_blocks * BLOCK)
     lane = lax.broadcasted_iota(jnp.int32, (1, WINDOW), 1)
 
-    group = {1: 8, 2: 4, 3: 2, 4: 2}[k_blocks]
+    group = {1: 8, 2: 8, 3: 4, 4: 8}[k_blocks]
 
     def several(i, carry):
         heads = []
@@ -167,23 +167,36 @@
             inside = jnp.logical_and(lane >= offset, lane < offset + HEAD_DIM)
             keep = jnp.where(inside, 1.0, 0.0).astype(jnp.bfloat16)
             heads.append((offset, window, keep))
-        probs_of, ds_of = [], []
-        for offset, window, keep in heads:
-            scores = dot(k_buf[k_rows, window] * keep, q_buf[q_rows, window], NT)
-            d_probs = dot(v_buf[k_rows, window] * keep, dm_buf[q_rows, window], NT)
+        def score(head):
+            offset, window, keep = head
+            return (
+                dot(k_buf[k_rows, window] * keep, q_buf[q_rows, window], NT),
+                dot(v_buf[k_rows, window] * keep, dm_buf[q_rows, window], NT),
+            )
+
+        def soften(scores, d_probs):
             top = jnp.max(scores, axis=0, keepdims=True)
             weights = jnp.exp2((scores - top) * EXP2_SCALE)
             probs = weights * (1.0 / jnp.sum(weights, axis=0, keepdims=True))
-            product = probs * d_probs
-            delta = jnp.sum(product, axis=0, keepdims=True)
-            probs_of.append(probs.astype(jnp.bfloat16))
-            ds_of.append((product - probs * delta).astype(jnp.bfloat16))
-        news = []
-        for (offset, window, keep), p, ds in zip(heads, probs_of, ds_of):
-            news.append((
+            probs_low = probs.astype(jnp.bfloat16)
+            delta = jnp.sum(probs * d_probs, axis=0, keepdims=True)
+            return probs_low, probs_low * (d_probs - delta).astype(jnp.bfloat16)
+
+        def combine(head, p, ds):
+            offset, window, keep = head
+            return (
                 dot(p, v_buf[k_rows, window], TN), dot(p, dm_buf[q_rows, window], NN),
                 dot(ds, k_buf[k_rows, window], TN) * SCALE, dot(ds, q_buf[q_rows, window], NN) * SCALE,
-            ))
+            )
+
+        news = []
+        raw = score(heads[0])
+        for at, head in enumerate(heads):
+            soft = soften(*raw)
+            if at + 1 < len(heads):
+                raw = score(heads[at + 1])
+            news.append(combine(head, *soft))
+
         for (offset, window, keep), new in zip(heads, news):
             for ref, rows, value in zip((mixed, gv, gq, gk), (q_rows, k_rows, q_rows, k_rows), new):
                 old = ref[rows, window]

time: 87.4 us -> 85.2 us (0.975); the launches traced: 87.2 us -> 83.6 us
  Pallas kernels: 86.4 us -> 82.8 us
    pallas_call x1, Pallas kernels: 23.6 us -> 20.5 us  [on_device(): pl.pallas_call(attention_kernel, out_shape=(mixed_shape, token_shape, tok...]
    pallas_call x1, Pallas kernels: 6.11 us -> 5.1 us  [on_device(): pl.pallas_call(functools.partial(settle_kernel, norm), out_shape=(token_s...]
where the time goes in v8:
time: 85.2 us; the launch traced here: 83.6 us
  Pallas kernels  82.8 us (97%)
    pallas_call x1, Pallas kernels, on_device(): pl.pallas_call(functools.partial(finish_kernel, count), out_shape=(halo_s...  40.3 us
    pallas_call x1, Pallas kernels, on_device(): pl.pallas_call(attention_kernel, out_shape=(mixed_shape, token_shape, tok...  20.5 us
    pallas_call x1, Pallas kernels, on_device(): pl.pallas_call(functools.partial(exchange_kernel, count), out_shape=(halo...  16.9 us
    pallas_call x1, Pallas kernels, on_device(): pl.pallas_call(functools.partial(settle_kernel, norm), out_shape=(token_s...  5.1 us

profile of v8, /device:TPU:64, one launch (start us, length us, event | category | flops | bytes accessed | tf_op | source)
XLA Modules:
  0.0 83.6 jit_solution(882194362564618436)
XLA Ops:
  0.6 16.9 %exchange.1 = (bf16[2,4,128,1152]{3,2,1,0:T(8,128)(2,1)}, bf16[512,1152]{1,0:T(8,128)(2,1)}) custom-call(s32[1,64]{1,0:T(1,128)} %lengths_ref.3, bf16[512,1152]{1,0:T(8,128)(2,1)} %bitcast.8, bf16[512,1152]{1,0:T(8,128)(2,1)} %bitcast.10, bf16[512,1152]{1,0:T(8,128)(2,1)} %bitcast.12, bf16[512,1152]{1,0:T(8,128)(2,1)} %bitcast.14, bf16[1152,1152]{1,0:T(8,128)(2,1)} %w_ref.5), custom_call_target="tpu_custom_call" | custom-call | tf_op jit(solution)/shard_map/exchange/pallas_call | solution.py:772
  17.6 20.5 %attention.1 = (bf16[768,1152]{1,0:T(8,128)(2,1)}, bf16[512,1152]{1,0:T(8,128)(2,1)}, bf16[512,1152]{1,0:T(8,128)(2,1)}, bf16[512,1152]{1,0:T(8,128)(2,1)}, bf16[2,4,128,1152]{3,2,1,0:T(8,128)(2,1)}, /*index=5*/s32[6]{0:T(128)}) custom-call(s32[1,64]{1,0:T(1,128)} %lengths_ref.3, bf16[512,1152]{1,0:T(8,128)(2,1)} %bitcast.9, bf16[512,1152]{1,0:T(8,128)(2,1)} %bitcast.11, ...), custom_call_target="tpu_custom_call" | custom-call | tf_op jit(solution)/shard_map/attention/pallas_call | solution.py:799
  38.0 40.3 %finish.1 = (bf16[2,4,128,1152]{3,2,1,0:T(8,128)(2,1)}, bf16[3,112,128]{2,1,0:T(8,128)(2,1)}, bf16[512,1152]{1,0:T(8,128)(2,1)}) custom-call(bf16[2,4,128,1152]{3,2,1,0:T(8,128)(2,1)} %get-tuple-element.24.ret_ref, bf16[768,1152]{1,0:T(8,128)(2,1)} %get-tuple-element.25.mixed_ref, bf16[512,1152]{1,0:T(8,128)(2,1)} %bitcast.15, ...), custom_call_target="tpu_custom_call" | custom-call | tf_op jit(solution)/shard_map/finish/pallas_call | solution.py:819
  78.3 5.1 %settle.1 = (bf16[512,1152]{1,0:T(8,128)(2,1)}, bf16[512,1152]{1,0:T(8,128)(2,1)}, bf16[512,1152]{1,0:T(8,128)(2,1)}, bf16[512,1152]{1,0:T(8,128)(2,1)}, f32[36,1152]{1,0:T(8,128)}) custom-call(s32[6]{0:T(128)} %get-tuple-element.23.flags_ref, ...), custom_call_target="tpu_custom_call", output_to_operand_aliasing={{1}: (4, {}), {2}: (5, {}), {3}: (6, {})} | custom-call | tf_op jit(solution)/shard_map/settle/pallas_call | solution.py:843
